TPU v7x, 32 devices: a whole 2x2x4 slice. The times are simulated.
32 devices in a mesh: dp: 8 (over z, y), ctx: 4 (over x, core).
Axes of the slice: x: 2, y: 2, z: 4, core: 2. Of those that a mesh axis runs over, the one named last changes fastest.
Arguments:
- tokens: bfloat16 [8192, 768], P(('dp', 'ctx')), may hold values from -12 to 12
- attn_gain: float32 [768], replicated, may hold values from 0.1 to 1.9
- attn_shift: float32 [768], replicated, may hold values from -3 to 3
- w_qkv: bfloat16 [768, 2304], replicated, may hold values from -0.21875 to 0.21875
- w_proj: bfloat16 [768, 768], replicated, may hold values from -1 to 1
- mlp_gain: float32 [768], replicated, may hold values from 0.1 to 1.9
- mlp_shift: float32 [768], replicated, may hold values from -3 to 3
- w_up: bfloat16 [768, 3072], replicated, may hold values from -0.21875 to 0.21875
- w_down: bfloat16 [3072, 768], replicated, may hold values from -0.109375 to 0.109375
- upstream: bfloat16 [8192, 768], P(('dp', 'ctx')), may hold values from -6 to 6
- clip_length: int32 [8], P('dp'), may hold values from 512 to 1024, as said below
- dataset_group: int32 [8, 1], P('dp'), may hold values from 0 to 3
- sample_weight: int32 [8], P('dp'), may hold values from 1 to 4
Outputs:
- block_out: bfloat16 [8192, 768], P(('dp', 'ctx'))
- input_grad: bfloat16 [8192, 768], P(('dp', 'ctx'))
- attn_gain_grad: float32 [768], P(('dp', 'ctx'))
- attn_shift_grad: float32 [768], P(('dp', 'ctx'))
- qkv_grad: float32 [768, 2304], P(('dp', 'ctx'))
- proj_grad: float32 [768, 768], P(('dp', 'ctx'))
- mlp_gain_grad: float32 [768], P(('dp', 'ctx'))
- mlp_shift_grad: float32 [768], P(('dp', 'ctx'))
- up_grad: float32 [768, 3072], P(('dp', 'ctx'))
- down_grad: float32 [3072, 768], P(('dp', 'ctx'))
Inputs may be any that keep to these rules, and one draw needn't show every extreme that they name: `clip_length`: some clip has exactly 1024 valid tokens and some exactly 512. `dataset_group`: every group names some clip.
All inputs are finite; a program needn't handle non-finite values.
Results may differ from a plain program's by a relative error of at most 0.015.
Values may be sent and summed in bfloat16 or wider, within the bound.
A program may use at most 192 MiB of HBM per device.

v0:
```python
import jax
import jax.numpy as jnp
from jax import lax
from jax.sharding import PartitionSpec as P

HD = 64
NGROUPS = 4


EPSILON = 1e-05
NEG_FILL = -1e30
GELU_COEF = 0.7978845608028654


def layer_norm(values, gain_vec, shift_vec):
    average = jnp.mean(values, axis=-1, keepdims=True)
    centred = values - average
    spread = jnp.mean(centred * centred, axis=-1, keepdims=True)
    return centred * lax.rsqrt(spread + EPSILON) * gain_vec + shift_vec


def gelu(inputs):
    return (
        0.5 * inputs * (1.0 + jnp.tanh(GELU_COEF * (inputs + 0.044715 * inputs * inputs * inputs)))
    )


def body(
    tokens,
    attn_gain,
    attn_shift,
    w_qkv,
    w_proj,
    mlp_gain,
    mlp_shift,
    w_up,
    w_down,
    upstream,
    clip_length,
    dataset_group,
    sample_weight,
):
    tok_rows = tokens.shape[0]
    model_width = tokens.shape[1]
    head_count = model_width // HD
    ctx_count = lax.axis_size("ctx")
    seq_rows = tok_rows * ctx_count
    first_row = lax.axis_index("ctx") * tok_rows
    length = clip_length[0]
    key_span = min(seq_rows, max(tok_rows, 512))
    block_count = seq_rows // key_span
    query_pos = first_row + jnp.arange(tok_rows, dtype=jnp.int32)
    last_pos = first_row + tok_rows - 1
    onehot = (dataset_group[0, 0] == jnp.arange(NGROUPS, dtype=jnp.int32)).astype(jnp.float32)
    counts = lax.psum(onehot * length.astype(jnp.float32), "dp")
    total_all = jnp.sum(counts)
    clip_scale = (
        sample_weight[0].astype(jnp.float32) * total_all / (NGROUPS * jnp.sum(onehot * counts))
    )
    x_rows = tokens.astype(jnp.float32)
    normed, norm_one_back = jax.vjp(layer_norm, x_rows, attn_gain, attn_shift)
    normed_low = normed.astype(jnp.bfloat16)
    mixed_qkv = jnp.dot(normed_low, w_qkv, preferred_element_type=jnp.float32).astype(jnp.bfloat16)
    queries = mixed_qkv[:, :model_width]
    key_local = mixed_qkv[:, model_width : 2 * model_width]
    value_local = mixed_qkv[:, 2 * model_width :]
    key_all, value_all = (
        lax.all_gather(key_local, "ctx", axis=0, tiled=True),
        lax.all_gather(value_local, "ctx", axis=0, tiled=True),
    )
    queries3 = queries.reshape(tok_rows, head_count, HD)

    def scores_for(kstart, key_rows):
        piece = key_rows[kstart : kstart + key_span].reshape(key_span, head_count, HD)
        raw = (
            jnp.einsum("qhd,khd->hqk", queries3, piece, preferred_element_type=jnp.float32) * 0.125
        )
        key_pos = kstart + jnp.arange(key_span, dtype=jnp.int32)
        allowed = (key_pos[None, :] <= query_pos[:, None]) & (key_pos[None, :] < length)
        return (jnp.where(allowed[None], raw, NEG_FILL), allowed)

    def useful(kstart):
        return (kstart <= last_pos) & (kstart < length)

    peak = jnp.full((head_count, tok_rows), NEG_FILL, jnp.float32)
    exp_total = jnp.zeros((head_count, tok_rows), jnp.float32)
    for index in range(block_count):
        kstart = index * key_span

        def gather_stats(carry, kstart=kstart):
            old_peak, old_total = carry
            scores, allowed = scores_for(kstart, key_all)
            new_peak = jnp.maximum(old_peak, jnp.max(scores, axis=-1))
            expo_vals = jnp.where(allowed[None], jnp.exp(scores - new_peak[..., None]), 0.0)
            return (
                new_peak,
                old_total * jnp.exp(old_peak - new_peak) + jnp.sum(expo_vals, axis=-1),
            )

        peak, exp_total = lax.cond(
            useful(kstart), gather_stats, lambda carry: carry, (peak, exp_total)
        )

    def probs_for(kstart, key_rows):
        scores, allowed = scores_for(kstart, key_rows)
        return (
            jnp.where(allowed[None], jnp.exp(scores - peak[..., None]), 0.0) / exp_total[..., None]
        )

    out_high = jnp.zeros((tok_rows, head_count, HD), jnp.float32)
    out_rest = jnp.zeros((tok_rows, head_count, HD), jnp.float32)
    for index in range(block_count):
        kstart = index * key_span

        def add_values(carry, kstart=kstart):
            high_acc, rest_acc = carry
            probs = probs_for(kstart, key_all)
            probs_low = probs.astype(jnp.bfloat16)
            remainder = (probs - probs_low.astype(jnp.float32)).astype(jnp.bfloat16)
            piece = value_all[kstart : kstart + key_span].reshape(key_span, head_count, HD)
            high_acc = high_acc + jnp.einsum(
                "hqk,khd->qhd", probs_low, piece, preferred_element_type=jnp.float32
            )
            rest_acc = rest_acc + jnp.einsum(
                "hqk,khd->qhd", remainder, piece, preferred_element_type=jnp.float32
            )
            return (high_acc, rest_acc)

        out_high, out_rest = lax.cond(
            useful(kstart), add_values, lambda carry: carry, (out_high, out_rest)
        )
    attended_low = out_high.reshape(tok_rows, model_width).astype(jnp.bfloat16)
    out_full = out_high + out_rest
    hidden = x_rows + jnp.dot(attended_low, w_proj, preferred_element_type=jnp.float32)
    normed_two, norm_two_back = jax.vjp(layer_norm, hidden, mlp_gain, mlp_shift)
    normed_two_low = normed_two.astype(jnp.bfloat16)
    up_proj = jnp.dot(normed_two_low, w_up, preferred_element_type=jnp.float32)
    gelu_vals, gelu_back = jax.vjp(gelu, up_proj)
    gelu_low = gelu_vals.astype(jnp.bfloat16)
    block_out = (hidden + jnp.dot(gelu_low, w_down, preferred_element_type=jnp.float32)).astype(
        jnp.bfloat16
    )
    valid = query_pos < length
    out_cot = upstream.astype(jnp.float32) * jnp.where(valid, clip_scale, 0.0)[:, None]
    out_cot_low = out_cot.astype(jnp.bfloat16)
    down_grad = jnp.einsum("tf,td->fd", gelu_low, out_cot_low, preferred_element_type=jnp.float32)
    gelu_in = jnp.einsum("td,fd->tf", out_cot_low, w_down, preferred_element_type=jnp.float32)
    (up_cot,) = gelu_back(gelu_in)
    up_cot_low = up_cot.astype(jnp.bfloat16)
    up_grad = jnp.einsum(
        "td,tf->df", normed_two_low, up_cot_low, preferred_element_type=jnp.float32
    )
    normed_two_cot = jnp.einsum("tf,df->td", up_cot_low, w_up, preferred_element_type=jnp.float32)
    norm_two_rows, mlp_gain_grad, mlp_shift_grad = norm_two_back(normed_two_cot)
    hidden_cot = out_cot + norm_two_rows
    hidden_cot_low = hidden_cot.astype(jnp.bfloat16)
    proj_grad = jnp.einsum(
        "ti,to->io", attended_low, hidden_cot_low, preferred_element_type=jnp.float32
    )
    attended_cot = jnp.einsum(
        "to,io->ti", hidden_cot_low, w_proj, preferred_element_type=jnp.float32
    ).astype(jnp.bfloat16)
    attended_cot3 = attended_cot.reshape(tok_rows, head_count, HD)
    delta = jnp.einsum("qhd,qhd->hq", attended_cot3.astype(jnp.float32), out_full)
    key_back, value_back = (key_all, value_all)
    query_cot = jnp.zeros((tok_rows, head_count, HD), jnp.float32)
    key_pieces = []
    value_pieces = []
    empty_piece = jnp.zeros((key_span, head_count, HD), jnp.float32)
    for index in range(block_count):
        kstart = index * key_span

        def block_grads(q_acc, kstart=kstart):
            probs = probs_for(kstart, key_back)
            probs_low = probs.astype(jnp.bfloat16)
            key_piece = key_back[kstart : kstart + key_span].reshape(key_span, head_count, HD)
            value_piece = value_back[kstart : kstart + key_span].reshape(key_span, head_count, HD)
            prob_cot = jnp.einsum(
                "qhd,khd->hqk", attended_cot3, value_piece, preferred_element_type=jnp.float32
            )
            score_cot = (probs * (prob_cot - delta[..., None])).astype(jnp.bfloat16)
            q_acc = (
                q_acc
                + jnp.einsum(
                    "hqk,khd->qhd", score_cot, key_piece, preferred_element_type=jnp.float32
                )
                * 0.125
            )
            key_term = (
                jnp.einsum("hqk,qhd->khd", score_cot, queries3, preferred_element_type=jnp.float32)
                * 0.125
            )
            value_term = jnp.einsum(
                "hqk,qhd->khd", probs_low, attended_cot3, preferred_element_type=jnp.float32
            )
            return (q_acc, key_term, value_term)

        query_cot, key_term, value_term = lax.cond(
            useful(kstart), block_grads, lambda q_acc: (q_acc, empty_piece, empty_piece), query_cot
        )
        key_pieces.append(key_term.reshape(key_span, model_width))
        value_pieces.append(value_term.reshape(key_span, model_width))
    key_terms = jnp.concatenate(key_pieces, axis=0)
    value_terms = jnp.concatenate(value_pieces, axis=0)
    key_cot, value_cot = (
        lax.psum_scatter(
            key_terms.astype(jnp.bfloat16), "ctx", scatter_dimension=0, tiled=True
        ).astype(jnp.float32),
        lax.psum_scatter(
            value_terms.astype(jnp.bfloat16), "ctx", scatter_dimension=0, tiled=True
        ).astype(jnp.float32),
    )
    mixed_cot = jnp.concatenate(
        [query_cot.reshape(tok_rows, model_width), key_cot, value_cot], axis=1
    ).astype(jnp.bfloat16)
    qkv_grad = jnp.einsum("td,te->de", normed_low, mixed_cot, preferred_element_type=jnp.float32)
    normed_cot = jnp.einsum("te,de->td", mixed_cot, w_qkv, preferred_element_type=jnp.float32)
    norm_one_rows, attn_gain_grad, attn_shift_grad = norm_one_back(normed_cot)
    input_grad = (hidden_cot + norm_one_rows).astype(jnp.bfloat16)
    reduced = (
        lax.psum_scatter(attn_gain_grad, ("dp", "ctx"), scatter_dimension=0, tiled=True),
        lax.psum_scatter(attn_shift_grad, ("dp", "ctx"), scatter_dimension=0, tiled=True),
        lax.psum_scatter(qkv_grad, ("dp", "ctx"), scatter_dimension=0, tiled=True),
        lax.psum_scatter(proj_grad, ("dp", "ctx"), scatter_dimension=0, tiled=True),
        lax.psum_scatter(mlp_gain_grad, ("dp", "ctx"), scatter_dimension=0, tiled=True),
        lax.psum_scatter(mlp_shift_grad, ("dp", "ctx"), scatter_dimension=0, tiled=True),
        lax.psum_scatter(up_grad, ("dp", "ctx"), scatter_dimension=0, tiled=True),
        lax.psum_scatter(down_grad, ("dp", "ctx"), scatter_dimension=0, tiled=True),
    )
    return (
        block_out,
        input_grad,
        reduced[0],
        reduced[1],
        reduced[2],
        reduced[3],
        reduced[4],
        reduced[5],
        reduced[6],
        reduced[7],
    )


def solution(mesh):
    in_specs = (
        P(("dp", "ctx"), None),
        P(),
        P(),
        P(),
        P(),
        P(),
        P(),
        P(),
        P(),
        P(("dp", "ctx"), None),
        P("dp"),
        P("dp", None),
        P("dp"),
    )
    out_specs = (
        P(("dp", "ctx"), None),
        P(("dp", "ctx"), None),
        P(("dp", "ctx")),
        P(("dp", "ctx")),
        P(("dp", "ctx"), None),
        P(("dp", "ctx"), None),
        P(("dp", "ctx")),
        P(("dp", "ctx")),
        P(("dp", "ctx"), None),
        P(("dp", "ctx"), None),
    )
    return jax.shard_map(body, mesh=mesh, in_specs=in_specs, out_specs=out_specs, check_vma=False)
```

profile of v0, /device:TPU:0, one launch (start us, length us, event | category | flops | bytes accessed | tf_op | source)
XLA Modules:
  0.0 783.0 jit_solution(10909269820325958576)
XLA Ops:
  8.9 23.1 %psum.7 = f32[4]{0:T(128)S(1)} all-reduce(f32[4]{0:T(128)S(1)} %compare_select_fusion.2), channel_id=1, replica_groups=mesh['dp'=8,'ctx'=4] {'dp'}, use_global_device_ids=true, to_apply=%region_16.17 | all-reduce | flops 4 | bytes 32 | tf_op jit(solution)/shard_map/psum | solution.py:55
  32.7 1.1 convert_reduce_fusion
  33.8 1.2 fusion.54
  37.6 2.2 convolution_convert_fusion
  39.8 1.0 fusion.81
  41.7 1.9 copy.53
  44.2 13.8 %all-gather.3.cloned.1.call-done = bf16[1024,768]{1,0:T(8,128)(2,1)} async-done(((bf16[256,768]{1,0:T(8,128)(2,1)}), bf16[1024,768]{1,0:T(8,128)(2,1)}) %all-gather.3.cloned.1.call-update) | async-done | bytes 1572880 | tf_op jit(solution)/shard_map/all_gather | solution.py:68
  57.9 11.6 %conditional.6 = (f32[12,256]{1,0:T(8,128)}, f32[12,256]{1,0:T(8,128)S(1)}) conditional(s32[]{:T(128)} %convert_element_type.116, () %tuple.83, (s32[256]{0:T(256)}, s32[]{:T(128)}, bf16[1024,768]{1,0:T(8,128)(2,1)}, bf16[256,12,64]{0,2,1:T(8,128)(2,1)}) %tuple.176), branch_computations={%region_2.0_spmd, %region_3.6_spmd} | conditional | flops 214181376 | bytes 19499056 | solution.py:100
  58.6 1.5 fusion.1
  60.1 2.6 copy.54
  62.7 1.2 slice.50
  63.9 2.3 fusion
  66.9 2.7 select_reduce_fusion
  69.6 10.2 %all-gather.5.cloned.1.call-done = bf16[1024,768]{1,0:T(8,128)(2,1)} async-done(((bf16[256,768]{1,0:T(8,128)(2,1)}), bf16[1024,768]{1,0:T(8,128)(2,1)}) %all-gather.5.cloned.1.call-update) | async-done | bytes 1572880 | tf_op jit(solution)/shard_map/all_gather | solution.py:69
  79.8 22.9 %conditional.8 = (f32[256,12,64]{0,2,1:T(8,128)}, f32[256,12,64]{0,2,1:T(8,128)}) conditional(s32[]{:T(128)} %convert_element_type.116, () %tuple.82, (s32[256]{0:T(256)}, s32[]{:T(128)}, bf16[1024,768]{1,0:T(8,128)(2,1)}, bf16[256,12,64]{0,2,1:T(8,128)(2,1)}, f32[12,256]{1,0:T(8,128)}, /*index=5*/f32[12,256]{1,0:T(8,128)S(1)}, ...), branch_computations={%region_10.11_spmd, %region_11.0_spmd} | conditional | flops 619971072 | bytes 58091568 | solution.py:129
  79.8 2.6 copy.56
  82.4 1.2 slice.52
  85.1 5.0 select_divide_fusion
  90.1 2.6 copy.57
  92.6 1.2 slice.53
  93.8 6.8 fusion.10
  100.6 2.0 fusion.7
  102.7 2.1 conditional.9
  102.7 1.9 convert_element_type.137
  104.8 2.2 fusion.82
  107.3 4.0 fusion.77
  111.4 4.7 fusion.41
  116.1 2.3 multiply_reduce_fusion
  120.6 1.2 convolution_convert_fusion.1
  121.9 1.9 copy.60
  123.8 1.6 fusion.57
  125.4 23.9 %conditional.10 = (f32[256,12,64]{0,2,1:T(8,128)}, bf16[512,768]{0,1:T(8,128)(2,1)}, bf16[512,768]{0,1:T(8,128)(2,1)}) conditional(s32[]{:T(128)} %convert_element_type.116, () %tuple.88, (s32[256]{0:T(256)}, s32[]{:T(128)}, bf16[1024,768]{1,0:T(8,128)(2,1)}, bf16[256,12,64]{0,2,1:T(8,128)(2,1)}, f32[12,256]{1,0:T(8,128)}, ...), branch_computations={%region_21.22_spmd, %region_22.23_spmd} | conditional | flops 1022427648 | bytes 72652984 | solution.py:198
  125.7 2.6 copy.61
  128.3 1.2 slice.54
  131.0 5.0 select_divide_fusion.1
  136.0 2.6 copy.62
  138.6 1.3 slice.55
  140.0 4.2 multiply_convert_fusion
  144.2 1.6 multiply_convert_fusion.1
  145.8 2.0 fusion.17
  147.8 1.6 fusion.14
  149.4 2.0 conditional.11
  151.3 2.7 pad_maximum_fusion
  154.1 2.7 pad_maximum_fusion.1
  157.0 3.0 fusion.83
  160.1 6.9 fusion.76
  167.3 1.9 convert.18
  169.2 62.1 %reduce-scatter.7.cloned.1.call-done = bf16[256,768]{0,1:T(8,128)(2,1)} async-done(((bf16[1024,768]{0,1:T(8,128)(2,1)}), bf16[256,768]{0,1:T(8,128)(2,1)}) %reduce-scatter.7.cloned.1.call-update) | async-done | bytes 393232 | tf_op jit(solution)/shard_map/reduce_scatter | solution.py:206
  231.4 30.7 %reduce-scatter.9.cloned.1.call-done = bf16[256,768]{0,1:T(8,128)(2,1)} async-done(((bf16[1024,768]{0,1:T(8,128)(2,1)}), bf16[256,768]{0,1:T(8,128)(2,1)}) %reduce-scatter.9.cloned.1.call-update) | async-done | bytes 393232 | tf_op jit(solution)/shard_map/reduce_scatter | solution.py:209
  262.1 5.6 fusion.59
  268.4 7.8 %fusion.62 = f32[3072,768]{1,0:T(8,128)} fusion(bf16[256,768]{1,0:T(8,128)(2,1)} %param.34, f32[256]{0:T(256)S(1)} %copy-done.38, f32[256,3072]{1,0:T(8,128)} %copy-done.9), kind=kOutput, calls=%fused_computation.110 | convolution fusion | flops 1215627264 | bytes 12977152 | tf_op jit(solution)/shard_map/tf,td->fd/dot_general | solution.py:146
  276.3 6.4 fusion.44
  282.7 1.8 fusion.78
  284.5 1.0 fusion.53
  285.6 40.1 %all-reduce.4 = (f32[768]{0:T(1024)}, f32[768]{0:T(1024)}, f32[768]{0:T(1024)}, f32[768]{0:T(1024)}) all-reduce(f32[768]{0:T(1024)} %get-tuple-element.391, f32[768]{0:T(1024)} %get-tuple-element.394, f32[768]{0:T(1024)} %get-tuple-element.389, f32[768]{0:T(1024)} %get-tuple-element.393), channel_id=4, replica_groups=mesh['dp'=8,'ctx'=4] {'dp','ctx'}, use_global_device_ids=true, to_apply=%region_30.31.clone | all-reduce | flops 3072 | bytes 24576
  325.7 1.3 dynamic-slice
  327.0 1.3 dynamic-slice.1
  328.2 1.3 dynamic-slice.2
  329.5 1.3 dynamic-slice.3
  331.4 2.8 add_convert_fusion
  334.2 32.8 %reduce-scatter.13.cloned.1.call-done = f32[24,768]{1,0:T(8,128)} async-done(((f32[768,768]{1,0:T(8,128)}), f32[24,768]{1,0:T(8,128)}) %reduce-scatter.13.cloned.1.call-update) | async-done | bytes 73744 | tf_op jit(solution)/shard_map/reduce_scatter | solution.py:224
  367.0 142.0 %reduce-scatter.15.cloned.1.call-done = f32[24,3072]{1,0:T(8,128)} async-done(((f32[768,3072]{1,0:T(8,128)}), f32[24,3072]{1,0:T(8,128)}) %reduce-scatter.15.cloned.1.call-update) | async-done | bytes 294928 | tf_op jit(solution)/shard_map/reduce_scatter | solution.py:227
  509.0 124.3 %reduce-scatter.11.cloned.1.call-done = f32[24,2304]{1,0:T(8,128)} async-done(((f32[768,2304]{1,0:T(8,128)}), f32[24,2304]{1,0:T(8,128)}) %reduce-scatter.11.cloned.1.call-update) | async-done | bytes 221200 | tf_op jit(solution)/shard_map/reduce_scatter | solution.py:223
  633.3 142.4 %reduce-scatter.17.cloned.1.call-done = f32[96,768]{1,0:T(8,128)} async-done(((f32[3072,768]{1,0:T(8,128)}), f32[96,768]{1,0:T(8,128)}) %reduce-scatter.17.cloned.1.call-update) | async-done | bytes 294928 | tf_op jit(solution)/shard_map/reduce_scatter | solution.py:228
  (135 shorter events, 13.3 us)
Async XLA Ops:
  7.2 30.4 %copy-start = (bf16[768,2304]{1,0:T(8,128)(2,1)S(1)}, bf16[768,2304]{1,0:T(8,128)(2,1)}, u32[]{:S(2)}) copy-start(bf16[768,2304]{1,0:T(8,128)(2,1)} %param.28) | copy-start | bytes 10616836
  7.2 50.7 %all-gather.3.cloned.1.call-start = ((), (), s32[]{:S(2)}) async-start(), calls=%async_computation.6 | async-start | bytes 1966080 | tf_op jit(solution)/shard_map/all_gather | solution.py:68
  33.8 6.0 copy-start.31
  35.1 4.7 copy-start.43
  37.6 2.2 copy-start.35
  40.9 38.9 %all-gather.5.cloned.1.call-start = ((), (), s32[]{:S(2)}) async-start(), calls=%async_computation.7 | async-start | bytes 1966080 | tf_op jit(solution)/shard_map/all_gather | solution.py:69
  41.6 189.8 %reduce-scatter.7.cloned.1.call-start = ((), (), s32[]{:S(2)}) async-start(), calls=%async_computation.8 | async-start | bytes 1966080 | tf_op jit(solution)/shard_map/reduce_scatter | solution.py:206
  63.9 3.0 copy-start.21
  69.6 33.1 %copy-start.30 = (f32[12,256]{1,0:T(8,128)}, f32[12,256]{1,0:T(8,128)S(1)}, u32[]{:S(2)}) copy-start(f32[12,256]{1,0:T(8,128)S(1)} %get-tuple-element.217) | copy-start | bytes 36868
  93.8 6.8 copy-start.1
  104.7 2.5 copy-start.25
  104.8 2.5 copy-start.27
  104.8 6.5 slice-start.6
  107.0 11.4 %copy-start.5 = (f32[256,768]{1,0:T(8,128)}, f32[256,768]{1,0:T(8,128)S(1)}, u32[]{:S(2)}) copy-start(f32[256,768]{1,0:T(8,128)S(1)} %get-tuple-element.414) | copy-start | bytes 2359300
  107.0 11.4 %copy-start.33 = (f32[256]{0:T(256)}, f32[256]{0:T(256)S(1)}, u32[]{:S(2)}) copy-start(f32[256]{0:T(256)S(1)} %broadcast_multiply_fusion) | copy-start | bytes 3076
  107.3 11.1 %copy-start.39 = (f32[256]{0:T(256)}, f32[256]{0:T(256)S(1)}, u32[]{:S(2)}) copy-start(f32[256]{0:T(256)S(1)} %fusion.69) | copy-start | bytes 3076
  107.3 4.0 copy-start.12
  107.3 4.0 copy-start.37
  107.3 4.0 slice-start.7
  107.3 8.7 %slice-start.4 = ((s8[4718592]{0:T(1024)(128)(4,1)}), s8[4194304]{0:T(1024)(128)(4,1)S(1)}, s32[]{:S(2)}) async-start(s8[4718592]{0:T(1024)(128)(4,1)} %bitcast.137), calls=%async_computation.18 | async-start | bytes 8388608
  111.3 4.7 copy-start.9
  111.3 4.7 slice-start.5
  116.1 2.3 copy-start.18
  118.4 2.2 copy-start.10
  118.8 0.9 copy-start.8
  118.8 1.1 copy-start.42
  119.9 0.8 copy-start.11
  129.5 6.6 copy-start.13
  138.6 9.1 %slice-start.2 = ((s8[6291456]{0:T(1024)(128)(4,1)}), s8[4194304]{0:T(1024)(128)(4,1)S(1)}, s32[]{:S(2)}) async-start(s8[6291456]{0:T(1024)(128)(4,1)} %bitcast.110), calls=%async_computation.16 | async-start | bytes 8388608 | tf_op jit(solution)/shard_map/cond
  140.0 4.2 copy-start.6
  140.0 7.8 slice-start.3
  144.2 1.6 copy-start.14
  145.8 2.0 copy-start.2
  154.1 108.0 %reduce-scatter.9.cloned.1.call-start = ((), (), s32[]{:S(2)}) async-start(), calls=%async_computation.9 | async-start | bytes 1966080 | tf_op jit(solution)/shard_map/reduce_scatter | solution.py:209
  156.9 3.2 copy-start.26
  156.9 3.1 copy-start.28
  156.9 3.1 copy-start.34
  156.9 3.1 copy-start.40
  156.9 210.1 %reduce-scatter.13.cloned.1.call-start = ((), (), s32[]{:S(2)}) async-start(), calls=%async_computation.11 | async-start | bytes 2433024 | tf_op jit(solution)/shard_map/reduce_scatter | solution.py:224
  160.0 349.0 %reduce-scatter.15.cloned.1.call-start = ((), (), s32[]{:S(2)}) async-start(), calls=%async_computation.12 | async-start | bytes 9732096 | tf_op jit(solution)/shard_map/reduce_scatter | solution.py:227
  167.0 95.1 %copy-start.24 = (f32[768]{0:T(1024)S(1)}, f32[768]{0:T(1024)}, u32[]{:S(2)}) copy-start(f32[768]{0:T(1024)} %param.26) | copy-start | bytes 9220
  167.0 95.1 %copy-start.29 = (f32[768]{0:T(1024)S(1)}, f32[768]{0:T(1024)}, u32[]{:S(2)}) copy-start(f32[768]{0:T(1024)} %param.27) | copy-start | bytes 9220
  167.0 95.1 %copy-start.32 = (f32[256]{0:T(256)S(1)}, f32[256]{0:T(256)}, u32[]{:S(2)}) copy-start(f32[256]{0:T(256)} %copy-done.31) | copy-start | bytes 3076
  167.0 95.1 %copy-start.36 = (f32[256]{0:T(256)S(1)}, f32[256]{0:T(256)}, u32[]{:S(2)}) copy-start(f32[256]{0:T(256)} %copy-done.35) | copy-start | bytes 3076
  167.0 466.3 %reduce-scatter.11.cloned.1.call-start = ((), (), s32[]{:S(2)}) async-start(), calls=%async_computation.10 | async-start | bytes 7299072 | tf_op jit(solution)/shard_map/reduce_scatter | solution.py:223
  267.7 0.7 copy-start.38
  267.8 508.0 %reduce-scatter.17.cloned.1.call-start = ((), (), s32[]{:S(2)}) async-start(), calls=%async_computation.13 | async-start | bytes 9732096 | tf_op jit(solution)/shard_map/reduce_scatter | solution.py:228
  276.3 6.4 copy-start.4
  276.3 6.4 copy-start.19
  276.3 6.4 copy-start.22
  276.3 6.4 copy-start.23
  282.7 1.8 copy-start.44
  284.5 1.1 copy-start.15
  284.5 1.1 copy-start.41
Sparse Core Ops, SparseCore 0:
  41.0 16.9 all-gather.2
  60.1 19.6 all-gather.4
  154.2 77.1 reduce-scatter.6
  233.9 28.1 reduce-scatter.8
  267.8 99.1 reduce-scatter.12
  374.3 134.6 reduce-scatter.14
  515.2 118.0 reduce-scatter.10
  640.8 134.9 reduce-scatter.16
where the time goes:
time: 793 us; the launch traced here: 783 us
  waiting for transfers between devices  559 us (70%)
  matrix products  78.5 us (10%)
  blocking collectives  63.3 us (8%)
  local copies, waits for them, and re-layouts  33.4 us (4%)
  other arithmetic  28.8 us (4%)
  between operations  18.8 us (2%)
    reduce_scatter x1, waiting for transfers between devices, body(): lax.psum_scatter(down_grad, ('dp', 'ctx'), scatter_dimension=0, tiled=True)  142 us
    reduce_scatter x1, waiting for transfers between devices, body(): lax.psum_scatter(up_grad, ('dp', 'ctx'), scatter_dimension=0, tiled=True)  142 us
    reduce_scatter x1, waiting for transfers between devices, body(): lax.psum_scatter(qkv_grad, ('dp', 'ctx'), scatter_dimension=0, tiled=True)  124 us
    reduce_scatter x1, waiting for transfers between devices, body(): lax.psum_scatter(key_terms.astype(jnp.bfloat16), 'ctx', scatter_dimension...  62.1 us
    unnamed x1, blocking collectives  40.1 us
    reduce_scatter x1, waiting for transfers between devices, body(): lax.psum_scatter(proj_grad, ('dp', 'ctx'), scatter_dimension=0, tiled=True)  32.8 us
    reduce_scatter x1, waiting for transfers between devices, body(): lax.psum_scatter(value_terms.astype(jnp.bfloat16), 'ctx', scatter_dimensi...  30.7 us
    psum x1, blocking collectives, body(): counts = lax.psum(onehot * length.astype(jnp.float32), 'dp')  23.1 us
  transfers between devices with their start and end apart: 8, of which 8 were waited for; matrix products, arithmetic and copies ran while one was open for 8% of the time, Pallas kernels for 0%

commit v1 on v0

--- a/solution.py
+++ b/solution.py
@@ -1,6 +1,8 @@
 import jax
 import jax.numpy as jnp
 from jax import lax
+from jax.experimental import pallas as pl
+from jax.experimental.pallas import tpu as pltpu
 from jax.sharding import PartitionSpec as P
 
 HD = 64
@@ -25,7 +27,650 @@
     )
 
 
-def body(
+MESH = pl.DeviceIdType.MESH
+BF16 = jnp.bfloat16
+F32 = jnp.float32
+ROWS = 256
+WIDTH = 768
+HIDDEN = 3072
+HALF_HEADS = 6
+HALF_WIDTH = 384
+BLOCKS = ((192, 384), (48, 1536), (48, 384), (48, 1152))
+
+
+def dot_nn(left, right):
+    return lax.dot_general(left, right, (((1,), (0,)), ((), ())), preferred_element_type=F32)
+
+
+def dot_nt(left, right):
+    return lax.dot_general(left, right, (((1,), (1,)), ((), ())), preferred_element_type=F32)
+
+
+def dot_tn(left, right):
+    return lax.dot_general(left, right, (((0,), (0,)), ((), ())), preferred_element_type=F32)
+
+
+def dot_tt(left, right):
+    return lax.dot_general(left, right, (((0,), (1,)), ((), ())), preferred_element_type=F32)
+
+
+def device_at(z, y, x, core):
+    return (z * 2 + y, x * 2 + core)
+
+
+def normalise(values):
+    average = jnp.mean(values, axis=-1, keepdims=True)
+    centred = values - average
+    spread = jnp.mean(centred * centred, axis=-1, keepdims=True)
+    inverse = lax.rsqrt(spread + EPSILON)
+    return centred * inverse, inverse
+
+
+def normalise_back(cot, gain, unit, inverse):
+    scaled = cot * gain
+    first = jnp.mean(scaled, axis=-1, keepdims=True)
+    second = jnp.mean(scaled * unit, axis=-1, keepdims=True)
+    return inverse * (scaled - first - unit * second)
+
+
+def loop(count, step):
+    def wrapped(index, carry):
+        step(index)
+        return carry
+
+    lax.fori_loop(0, count, wrapped, 0)
+
+
+def at(start, size, unit):
+    return pl.ds(pl.multiple_of(start, unit), size)
+
+
+def layer_kernel(
+    length_ref, group_ref, weight_ref, tok, ups, gain1, shift1, gain2, shift2,
+    w_qkv, w_proj, w_up, w_down,
+    block_out, input_grad, o_v0, o_v1, o_qk, o_pr, o_v2, o_v3, o_up, o_dn,
+    wq, wp, wu, wd, tokc, tokf, nc, nf, qkvt, kvft, bias, ec, ef, o1, m1, l1, f1, f2,
+    attt, hid, n2, gel, dg, outl, outh, upo, uph, ncot, hc, hl, mixc, mixf,
+    cs, cr, vsend, vrecv,
+    g_dn, g_up, g_pr, g_qk,
+    r1_dn, r1_up, r1_pr, r1_qk, s2_dn, s2_up, s2_pr, s2_qk, r2_dn, r2_up, r2_pr, r2_qk,
+    s3_dn, s3_up, s3_pr, s3_qk, r3_dn, r3_up, r3_pr, r3_qk, f_dn, f_up, f_pr, f_qk,
+    send_sem, recv_sem, misc_send, misc_recv, local_sem,
+):
+    dp, ctx = lax.axis_index("dp"), lax.axis_index("ctx")
+    z, y, x, core = dp // 2, dp % 2, ctx // 2, ctx % 2
+    mate = device_at(z, y, x, 1 - core)
+    x_peer = device_at(z, y, 1 - x, core)
+    y_peer = device_at(z, 1 - y, x, core)
+    z_peers = [device_at((z + d) % 4, y, x, core) for d in (1, 2, 3)]
+    own, oth = core * ROWS, (1 - core) * ROWS
+    own_rows, oth_rows = at(own, ROWS, ROWS), at(oth, ROWS, ROWS)
+    own_half, oth_half = at(core * HALF_WIDTH, HALF_WIDTH, 128), at((1 - core) * HALF_WIDTH, HALF_WIDTH, 128)
+    length, group = length_ref[0], group_ref[0]
+    left, right = x == 0, x == 1
+
+    def fetch(slot, src, dst):
+        return pltpu.make_async_copy(src, dst, local_sem.at[slot])
+
+    def weight_copies(name):
+        if name == "qkv":
+            return [
+                fetch(i, w_qkv.at[:, at(i * WIDTH + core * HALF_WIDTH, HALF_WIDTH, 128)],
+                      wq.at[:, pl.ds(i * HALF_WIDTH, HALF_WIDTH)])
+                for i in range(3)
+            ]
+        if name == "proj":
+            return [fetch(3, w_proj, wp)]
+        if name == "up":
+            return [fetch(4, w_up, wu)]
+        return [fetch(5, w_down, wd)]
+
+    for name in ("qkv", "proj", "up", "down"):
+        for copy in weight_copies(name):
+            copy.start()
+
+    def arrive(name):
+        for copy in weight_copies(name):
+            copy.wait()
+
+    peers = [mate, x_peer, y_peer] + z_peers
+    barrier = pltpu.get_barrier_semaphore()
+    for peer in peers:
+        pl.semaphore_signal(barrier, inc=1, device_id=peer, device_id_type=MESH)
+    pl.semaphore_wait(barrier, len(peers))
+
+    def misc(slot, src, dst, target):
+        return pltpu.make_async_remote_copy(
+            src_ref=src, dst_ref=dst, send_sem=misc_send.at[slot], recv_sem=misc_recv.at[slot],
+            device_id=target, device_id_type=MESH,
+        )
+
+    tok_far = misc(0, tok, tokf.at[own_rows], x_peer)
+    tok_mate = misc(1, tok, tokc.at[own_rows], mate)
+    tok_on = misc(2, tokf.at[own_rows], tokf.at[own_rows], mate)
+    ups_mate = misc(3, ups.at[:, oth_half], outh.at[own_rows], mate)
+    count_y = misc(4, cs.at[0], cr.at[0], y_peer)
+    count_z = [misc(4 + d, cs.at[1], cr.at[d], z_peers[d - 1]) for d in (1, 2, 3)]
+    att_rows = at(core * HALF_WIDTH, HALF_WIDTH, 128)
+    att_mate = misc(8, attt.at[att_rows], attt.at[att_rows], mate)
+    n2_mate = misc(9, n2.at[own_rows], n2.at[own_rows], mate)
+    gel_mate = [
+        misc(10 + i, gel.at[own_rows, pl.ds(1024 * i, 1024)], gel.at[own_rows, pl.ds(1024 * i, 1024)], mate)
+        for i in range(3)
+    ]
+    up_mate = misc(13, upo.at[:, at((1 - core) * 1536, 1536, 128)], uph.at[own_rows], mate)
+    hl_mate = misc(14, hl.at[own_rows], hl.at[own_rows], mate)
+    nc_mate = misc(15, tokc.at[own_rows], tokc.at[own_rows], mate)
+    nf_mate = misc(16, tokf.at[own_rows], tokf.at[own_rows], mate)
+    nf_far = misc(17, tokf.at[own_rows], tokf.at[own_rows], x_peer)
+
+    @pl.when(left)
+    def _():
+        tok_far.start()
+
+    tok_mate.start()
+    ups_mate.start()
+    lane = lax.broadcasted_iota(jnp.int32, (8, 128), 1)
+    cs[0] = jnp.where(lane == group, length.astype(F32), 0.0)
+    count_y.start()
+
+    def first_norm(src, src_at, dst, dst_at):
+        def step(i):
+            unit, _ = normalise(src[at(src_at + i * 64, 64, 64), :].astype(F32))
+            dst[at(dst_at + i * 64, 64, 64), :] = (unit * gain1[...] + shift1[...]).astype(BF16)
+
+        loop(ROWS // 64, step)
+
+    first_norm(tok, 0, nc, own)
+    tok_mate.wait()
+    first_norm(tokc, oth, nc, oth)
+    arrive("qkv")
+
+    def project(i):
+        part = dot_tt(wq[:, at(i * HALF_WIDTH, HALF_WIDTH, 128)], nc[...])
+        qkvt[at(i * HALF_WIDTH, HALF_WIDTH, 128), :] = (part * jnp.where(i == 0, 0.125, 1.0)).astype(BF16)
+
+    loop(3, project)
+
+    key_at = lax.broadcasted_iota(jnp.int32, (512, 512), 0)
+    query_at = lax.broadcasted_iota(jnp.int32, (512, 512), 1)
+    bias[...] = jnp.where((key_at <= query_at) & (key_at + x * 512 < length), 0.0, NEG_FILL).astype(BF16)
+
+    def attend_chip(h):
+        r = h * 64
+        keys, queries, values = qkvt[at(HALF_WIDTH + r, 64, 64), :], qkvt[at(r, 64, 64), :], qkvt[at(2 * HALF_WIDTH + r, 64, 64), :]
+        for half in (0, 1):
+            span, cols = 256 * (half + 1), slice(256 * half, 256 * half + 256)
+            scores = dot_tn(keys[:, :span], queries[:, cols]) + bias[:span, cols].astype(F32)
+            peak = jnp.max(scores, axis=0, keepdims=True)
+            expo = jnp.exp(scores - peak)
+            expo_low = expo.astype(BF16)
+            m1[pl.ds(h, 1), cols] = peak
+            l1[pl.ds(h, 1), cols] = jnp.sum(expo_low.astype(F32), axis=0, keepdims=True)
+            ec[h, :span, cols] = expo_low
+            o1[at(r, 64, 64), cols] = dot_nn(values[:, :span], expo_low)
+
+    loop(HALF_HEADS, attend_chip)
+
+    count_y.wait()
+    cs[1] = cs[0] + cr[0]
+    for copy in count_z:
+        copy.start()
+    for copy in count_z:
+        copy.wait()
+    counts = cs[1] + cr[1] + cr[2] + cr[3]
+    total = jnp.sum(counts, axis=1, keepdims=True)
+    mine = jnp.sum(jnp.where(lane == group, counts, 0.0), axis=1, keepdims=True)
+    scale = (weight_ref[0].astype(F32) * total / (NGROUPS * mine))[0:1, 0:1]
+    row_at = lax.broadcasted_iota(jnp.int32, (ROWS, 1), 0) + x * 512
+    own_scale = jnp.where(row_at + own < length, scale, 0.0)
+    oth_scale = jnp.where(row_at + oth < length, scale, 0.0)
+    outl[...] = (ups[...].astype(F32) * own_scale).astype(BF16)
+    outh[own_rows, :] = (ups[:, own_half].astype(F32) * own_scale).astype(BF16)
+    ups_mate.wait()
+    outh[oth_rows, :] = (outh[oth_rows, :].astype(F32) * oth_scale).astype(BF16)
+
+    @pl.when(right)
+    def _():
+        def far_block(start):
+            first_norm(tokf, start, nf, start)
+            columns = at(start, ROWS, ROWS)
+
+            def project_far(i):
+                part = dot_tt(wq[:, at((i + 1) * HALF_WIDTH, HALF_WIDTH, 128)], nf[columns, :])
+                kvft[at(i * HALF_WIDTH, HALF_WIDTH, 128), columns] = part.astype(BF16)
+
+            loop(2, project_far)
+
+        tok_far.wait_recv()
+        tok_on.start()
+        far_block(own)
+        tok_on.wait()
+        far_block(oth)
+
+        def attend_far(h):
+            r = h * 64
+            keys, queries, values = kvft[at(r, 64, 64), :], qkvt[at(r, 64, 64), :], kvft[at(HALF_WIDTH + r, 64, 64), :]
+            for half in (0, 1):
+                cols = slice(256 * half, 256 * half + 256)
+                scores = dot_tn(keys, queries[:, cols])
+                peak = jnp.max(scores, axis=0, keepdims=True)
+                expo = jnp.exp(scores - peak)
+                expo_low = expo.astype(BF16)
+                expo_sum = jnp.sum(expo_low.astype(F32), axis=0, keepdims=True)
+                ef[h, :, cols] = expo_low
+                out = dot_nn(values, expo_low)
+                old = m1[pl.ds(h, 1), cols]
+                top = jnp.maximum(old, peak)
+                old_part, new_part = jnp.exp(old - top), jnp.exp(peak - top)
+                share = 1.0 / (l1[pl.ds(h, 1), cols] * old_part + expo_sum * new_part)
+                f1[pl.ds(h, 1), cols] = old_part * share
+                f2[pl.ds(h, 1), cols] = new_part * share
+                o1[at(r, 64, 64), cols] = o1[at(r, 64, 64), cols] * (old_part * share) + out * (new_part * share)
+
+        loop(HALF_HEADS, attend_far)
+
+    @pl.when(left)
+    def _():
+        nf[...] = jnp.zeros_like(nf)
+        mixf[...] = jnp.zeros_like(mixf)
+
+        def share_out(h):
+            share = 1.0 / l1[pl.ds(h, 1), :]
+            f1[pl.ds(h, 1), :] = share
+            f2[pl.ds(h, 1), :] = jnp.zeros_like(share)
+            o1[at(h * 64, 64, 64), :] = o1[at(h * 64, 64, 64), :] * share
+
+        loop(HALF_HEADS, share_out)
+
+    attt[att_rows, :] = o1[...].astype(BF16)
+    att_mate.start()
+    arrive("proj")
+    att_mate.wait()
+
+    for i in range(3):
+        cols = slice(256 * i, 256 * i + 256)
+        hid[:, cols] = tok[:, cols].astype(F32) + dot_tn(attt[:, own_rows], wp[:, cols])
+
+    def second_norm(i):
+        unit, _ = normalise(hid[at(i * 64, 64, 64), :])
+        n2[at(own + i * 64, 64, 64), :] = (unit * gain2[...] + shift2[...]).astype(BF16)
+
+    loop(ROWS // 64, second_norm)
+    n2_mate.start()
+    arrive("up")
+    for part in range(3):
+
+        def feed(i, part=part):
+            cols = at(part * 1024 + i * 256, 256, 256)
+            u = dot_nn(n2[own_rows, :], wu[:, cols])
+            square = u * u
+            bend = jnp.tanh(GELU_COEF * (u + 0.044715 * square * u))
+            lift = 0.5 * (1.0 + bend)
+            gel[own_rows, cols] = (u * lift).astype(BF16)
+            slope = lift + 0.5 * u * (1.0 - bend * bend) * (GELU_COEF * (1.0 + 3 * 0.044715 * square))
+            dg[:, cols] = slope.astype(BF16)
+
+        loop(4, feed)
+        gel_mate[part].start()
+
+    first = device_at(z, (y + core) % 2, (x + 1 - core) % 2, core)
+    second = device_at(z, (y + 1 - core) % 2, (x + core) % 2, core)
+    kept = jnp.where(core == 0, y, x)
+    grads = (g_dn, g_up, g_pr, g_qk)
+    outs = (o_dn, o_up, o_pr, o_qk)
+    r1s, s2s, r2s = (r1_dn, r1_up, r1_pr, r1_qk), (s2_dn, s2_up, s2_pr, s2_qk), (r2_dn, r2_up, r2_pr, r2_qk)
+    s3s, r3s = (s3_dn, s3_up, s3_pr, s3_qk), (r3_dn, r3_up, r3_pr, r3_qk)
+    fs = (f_dn, f_up, f_pr, f_qk)
+
+    def remote(src, dst, w, slot, target):
+        return pltpu.make_async_remote_copy(
+            src_ref=src, dst_ref=dst, send_sem=send_sem.at[w, slot], recv_sem=recv_sem.at[w, slot],
+            device_id=target, device_id_type=MESH,
+        )
+
+    def block(w, index):
+        rows = BLOCKS[w][0]
+        return at(index * rows, rows, 16)
+
+    def kept_block(w, zz, j):
+        return grads[w][block(w, zz * 4 + jnp.where(core == 0, j * 2 + x, y * 2 + j)), :].astype(F32)
+
+    def first_copy(w, zz, j):
+        index = zz * 4 + jnp.where(core == 0, j * 2 + 1 - x, (1 - y) * 2 + j)
+        return remote(grads[w].at[block(w, index)], r1s[w].at[zz, j], w, zz * 2 + j, first)
+
+    def start_first(w, places):
+        for zz in places:
+            for j in range(2):
+                first_copy(w, zz, j).start()
+
+    def second_copy(w):
+        return remote(s2s[w], r2s[w], w, 8, second)
+
+    def third_copy(w, d):
+        return remote(s3s[w].at[d - 1], r3s[w].at[d - 1], w, 8 + d, z_peers[d - 1])
+
+    def places(w):
+        parts = 3 if w == 3 else 1
+        width = BLOCKS[w][1] // parts
+        return [(pl.ds(i * width, width), at((2 * i + core) * width, width, 128)) for i in range(parts)]
+
+    def last_copies(w):
+        rows = BLOCKS[w][0] // 2
+        far_rows = at((1 - core) * rows, rows, 8)
+        return [
+            remote(fs[w].at[far_rows, src], outs[w].at[:, dst], w, 12 + i, mate)
+            for i, (src, dst) in enumerate(places(w))
+        ]
+
+    def start_second(w):
+        for zz in range(4):
+            for j in range(2):
+                first_copy(w, zz, j).wait()
+        j = 1 - kept
+        for zz in range(4):
+            s2s[w][zz] = (kept_block(w, zz, j) + r1s[w][zz, j].astype(F32)).astype(BF16)
+        second_copy(w).start()
+
+    def summed(w, zz):
+        return kept_block(w, zz, kept) + r1s[w][zz, kept].astype(F32) + r2s[w][zz].astype(F32)
+
+    def start_third(w):
+        second_copy(w).wait()
+        for d in (1, 2, 3):
+            s3s[w][d - 1] = summed(w, (z + d) % 4).astype(BF16)
+            third_copy(w, d).start()
+        fs[w][...] = summed(w, z)
+
+    def start_last(w):
+        for d in (1, 2, 3):
+            third_copy(w, d).wait()
+        rows = BLOCKS[w][0] // 2
+        fs[w][...] = fs[w][...] + r3s[w][0].astype(F32) + r3s[w][1].astype(F32) + r3s[w][2].astype(F32)
+        for copy in last_copies(w):
+            copy.start()
+        for src, dst in places(w):
+            outs[w][:, dst] = fs[w][at(core * rows, rows, 8), src]
+
+    def finish(w):
+        for copy in last_copies(w):
+            copy.wait()
+
+    for copy in gel_mate:
+        copy.wait()
+    for zz in range(4):
+
+        def down_rows(i, zz=zz):
+            start = zz * WIDTH + i * 256
+            g_dn[at(start, 256, 256), :] = dot_tn(gel[:, at(start, 256, 256)], outh[...]).astype(BF16)
+
+        loop(3, down_rows)
+        start_first(0, (zz,))
+
+    arrive("down")
+
+    def gelu_back(cols):
+        up_cot = dot_nt(outl[...], wd[cols, :]) * dg[:, cols].astype(F32)
+        up_cot = up_cot.astype(BF16)
+        upo[:, cols] = up_cot
+        return up_cot
+
+    def back_other(i):
+        gelu_back(at((1 - core) * 1536 + i * 256, 256, 256))
+
+    def back_own(i):
+        uph[own_rows, at(i * 256, 256, 256)] = gelu_back(at(core * 1536 + i * 256, 256, 256))
+
+    loop(6, back_other)
+    up_mate.start()
+    loop(6, back_own)
+
+    def n2_back(i):
+        cols = at(i * 256, 256, 256)
+        ncot[:, cols] = dot_nt(upo[...], wu[cols, :])
+
+    loop(3, n2_back)
+    vsend[...] = jnp.zeros_like(vsend)
+
+    def second_back(i):
+        rows = at(i * 64, 64, 64)
+        unit, inverse = normalise(hid[rows, :])
+        cot = ncot[rows, :]
+        position = lax.broadcasted_iota(jnp.int32, (64, 1), 0) + i * 64 + x * 512 + own
+        out_cot = ups[rows, :].astype(F32) * jnp.where(position < length, scale, 0.0)
+        hidden_cot = out_cot + normalise_back(cot, gain2[...], unit, inverse)
+        hc[rows, :] = hidden_cot
+        hl[at(own + i * 64, 64, 64), :] = hidden_cot.astype(BF16)
+        vsend[0, 2:3, :] += jnp.sum(cot * unit, axis=0, keepdims=True)
+        vsend[0, 3:4, :] += jnp.sum(cot, axis=0, keepdims=True)
+
+    loop(ROWS // 64, second_back)
+    hl_mate.start()
+
+    n2_mate.wait()
+    up_mate.wait()
+    for part in range(2):
+
+        def up_columns(i, part=part):
+            cols = at(i * 512, 512, 512)
+            g_up[384 * part : 384 * part + 384, cols] = dot_tn(n2[:, 384 * part : 384 * part + 384], uph[:, cols]).astype(BF16)
+
+        loop(3, up_columns)
+        start_first(1, (2 * part, 2 * part + 1))
+
+    hl_mate.wait()
+
+    def proj_rows(i):
+        rows = at(i * 256, 256, 256)
+        g_pr[rows, :] = dot_nn(attt[rows, :], hl[:, own_half]).astype(BF16)
+
+    loop(3, proj_rows)
+    start_first(2, range(4))
+    attt[att_rows, :] = dot_nt(wp[att_rows, :], hl[...]).astype(BF16)
+
+    def attend_back(h):
+        r = h * 64
+        rows = at(r, 64, 64)
+        keys, queries, values = qkvt[at(HALF_WIDTH + r, 64, 64), :], qkvt[rows, :], qkvt[at(2 * HALF_WIDTH + r, 64, 64), :]
+        cot = attt[at(core * HALF_WIDTH + r, 64, 64), :].astype(F32)
+        near = (cot * f1[pl.ds(h, 1), :]).astype(BF16)
+        delta = jnp.sum(near.astype(F32) * o1[rows, :], axis=0, keepdims=True)
+        far = (cot * f2[pl.ds(h, 1), :]).astype(BF16)
+        far_delta = jnp.sum(far.astype(F32) * o1[rows, :], axis=0, keepdims=True)
+        key_terms, value_terms = [], []
+        for half in (0, 1):
+            span, cols = 256 * (half + 1), slice(256 * half, 256 * half + 256)
+            expo = ec[h, :span, cols]
+            prob_cot = dot_tn(values[:, :span], near[:, cols])
+            score_cot = (expo.astype(F32) * (prob_cot - delta[:, cols])).astype(BF16)
+            o1[rows, cols] = dot_nn(keys[:, :span], score_cot)
+            key_terms.append(dot_nt(queries[:, cols], score_cot))
+            value_terms.append(dot_nt(near[:, cols], expo))
+        for start, terms in ((HALF_WIDTH, key_terms), (2 * HALF_WIDTH, value_terms)):
+            mixc[at(start + r, 64, 64), :256] = (terms[0] + terms[1][:, :256]).astype(BF16)
+            mixc[at(start + r, 64, 64), 256:] = terms[1][:, 256:].astype(BF16)
+
+        @pl.when(right)
+        def _():
+            far_keys, far_values = kvft[rows, :], kvft[at(HALF_WIDTH + r, 64, 64), :]
+            expo = ef[h]
+            prob_cot = dot_tn(far_values, far)
+            score_cot = (expo.astype(F32) * (prob_cot - far_delta)).astype(BF16)
+            o1[rows, :] += dot_nn(far_keys, score_cot)
+            mixf[rows, :] = dot_nt(queries, score_cot).astype(BF16)
+            mixf[at(HALF_WIDTH + r, 64, 64), :] = dot_nt(far, expo).astype(BF16)
+
+        mixc[rows, :] = (o1[rows, :] * 0.125).astype(BF16)
+
+    def attend_back_late(h):
+        attend_back(h + 3)
+
+    loop(3, attend_back)
+    start_second(0)
+    loop(3, attend_back_late)
+    start_second(1)
+
+    def normed_cot(mixed, first_column, columns, store):
+        def step(i):
+            rows = at(i * 256, 256, 256)
+            store(rows, dot_tt(mixed[:, columns], wq[rows, first_column:]))
+
+        loop(3, step)
+
+    def store_to(ref, rows):
+        def store(cols, value):
+            ref[rows, cols] = value.astype(ref.dtype)
+
+        return store
+
+    @pl.when(right)
+    def _():
+        normed_cot(mixf, HALF_WIDTH, oth_rows, store_to(tokf, own_rows))
+        nf_mate.start()
+
+    normed_cot(mixc, 0, oth_rows, store_to(tokc, own_rows))
+    nc_mate.start()
+
+    @pl.when(right)
+    def _():
+        normed_cot(mixf, HALF_WIDTH, own_rows, store_to(ncot, at(0, ROWS, ROWS)))
+        nf_mate.wait()
+        tokf[own_rows, :] = (ncot[...] + tokf[oth_rows, :].astype(F32)).astype(BF16)
+        nf_far.start()
+
+    for part in range(2):
+        cols = slice(384 * part, 384 * part + 384)
+        g_qk[cols, :384] = dot_tt(nc[:, cols], mixc[:384, :]).astype(BF16)
+        for i in range(2):
+            g_qk[cols, 384 * (i + 1) : 384 * (i + 2)] = (
+                dot_tt(nc[:, cols], mixc[384 * (i + 1) : 384 * (i + 2), :])
+                + dot_tt(nf[:, cols], mixf[384 * i : 384 * (i + 1), :])
+            ).astype(BF16)
+        start_first(3, (2 * part, 2 * part + 1))
+
+    normed_cot(mixc, 0, own_rows, store_to(ncot, at(0, ROWS, ROWS)))
+    start_third(0)
+    start_second(2)
+
+    def block_rows(i):
+        cols = at(i * 256, 256, 256)
+        block_out[:, cols] = (hid[:, cols] + dot_nn(gel[own_rows, :], wd[:, cols])).astype(BF16)
+
+    loop(3, block_rows)
+    nc_mate.wait()
+
+    @pl.when(left)
+    def _():
+        nf_far.wait_recv()
+        tok_far.wait_send()
+
+    @pl.when(right)
+    def _():
+        nf_far.wait_send()
+
+    def first_back(i):
+        rows = at(i * 64, 64, 64)
+        unit, inverse = normalise(tok[rows, :].astype(F32))
+        near = tokc[at(oth + i * 64, 64, 64), :].astype(F32)
+        far = tokf[at(own + i * 64, 64, 64), :].astype(F32)
+        cot = ncot[rows, :] + near + jnp.where(left, far, 0.0)
+        input_grad[rows, :] = (hc[rows, :] + normalise_back(cot, gain1[...], unit, inverse)).astype(BF16)
+        vsend[0, 0:1, :] += jnp.sum(cot * unit, axis=0, keepdims=True)
+        vsend[0, 1:2, :] += jnp.sum(cot, axis=0, keepdims=True)
+
+    loop(ROWS // 64, first_back)
+
+    def vector_copy(slot, target):
+        return misc(18 + slot, vsend.at[min(slot, 3)], vrecv.at[slot], target)
+
+    vector_copy(0, mate).start()
+    start_third(1)
+    vector_copy(0, mate).wait()
+    vsend[1] = vsend[0] + vrecv[0]
+    vector_copy(1, x_peer).start()
+    start_second(3)
+    vector_copy(1, x_peer).wait()
+    vsend[2] = vsend[1] + vrecv[1]
+    vector_copy(2, y_peer).start()
+    start_last(0)
+    start_third(2)
+    vector_copy(2, y_peer).wait()
+    vsend[3] = vsend[2] + vrecv[2]
+    for d in (1, 2, 3):
+        vector_copy(2 + d, z_peers[d - 1]).start()
+    start_last(1)
+    start_third(3)
+    for d in (1, 2, 3):
+        vector_copy(2 + d, z_peers[d - 1]).wait()
+    sums = vsend[3] + vrecv[3] + vrecv[4] + vrecv[5]
+    rank = dp * 4 + ctx
+    sums = pltpu.roll(sums, lax.rem(WIDTH - rank * 24, WIDTH), 1)
+    for i, ref in enumerate((o_v0, o_v1, o_v2, o_v3)):
+        ref[...] = sums[i : i + 1, :128]
+    start_last(2)
+    start_last(3)
+    for w in range(4):
+        finish(w)
+
+
+def fused_layer(args):
+    vmem, smem, anywhere = (
+        pl.BlockSpec(memory_space=pltpu.VMEM),
+        pl.BlockSpec(memory_space=pltpu.SMEM),
+        pl.BlockSpec(memory_space=pl.ANY),
+    )
+
+    def low(*shape):
+        return pltpu.VMEM(shape, BF16)
+
+    def full(*shape):
+        return pltpu.VMEM(shape, F32)
+
+    def per_block(lead):
+        return [pltpu.VMEM(lead + block, BF16) for block in BLOCKS]
+
+    vector = jax.ShapeDtypeStruct((1, 128), F32)
+
+    def grad_shape(w):
+        return jax.ShapeDtypeStruct((BLOCKS[w][0] // 2, BLOCKS[w][1] * 2), F32)
+
+    rows_out = jax.ShapeDtypeStruct((ROWS, WIDTH), BF16)
+    return pl.pallas_call(
+        layer_kernel,
+        out_shape=[
+            rows_out, rows_out, vector, vector, grad_shape(3), grad_shape(2), vector, vector,
+            grad_shape(1), grad_shape(0),
+        ],
+        in_specs=[smem] * 3 + [vmem] * 6 + [anywhere] * 4,
+        out_specs=[vmem] * 10,
+        scratch_shapes=[
+            low(768, 1152), low(768, 768), low(768, 3072), low(3072, 768),
+            low(512, 768), low(512, 768), low(512, 768), low(512, 768),
+            low(1152, 512), low(768, 512), low(512, 512), low(6, 512, 512), low(6, 512, 512),
+            full(384, 512), full(8, 512), full(8, 512), full(8, 512), full(8, 512),
+            low(768, 512), full(256, 768), low(512, 768), low(512, 3072), low(256, 3072),
+            low(256, 768), low(512, 384), low(256, 3072), low(512, 1536), full(256, 768),
+            full(256, 768), low(512, 768), low(1152, 512), low(768, 512),
+            full(2, 8, 128), full(4, 8, 128), full(4, 8, 768), full(6, 8, 768),
+            low(3072, 384), low(768, 1536), low(768, 384), low(768, 1152),
+        ]
+        + per_block((4, 2)) + per_block((4,)) + per_block((4,)) + per_block((3,)) + per_block((3,))
+        + [pltpu.VMEM(block, F32) for block in BLOCKS]
+        + [
+            pltpu.SemaphoreType.DMA((4, 15)),
+            pltpu.SemaphoreType.DMA((4, 15)),
+            pltpu.SemaphoreType.DMA((24,)),
+            pltpu.SemaphoreType.DMA((24,)),
+            pltpu.SemaphoreType.DMA((6,)),
+        ],
+        compiler_params=pltpu.CompilerParams(
+            collective_id=0, has_side_effects=True, vmem_limit_bytes=60 * 1024 * 1024
+        ),
+    )(*args)
+
+
+def general_body(
     tokens,
     attn_gain,
     attn_shift,
@@ -241,6 +886,19 @@
     )
 
 
+def fused_body(
+    tokens, attn_gain, attn_shift, w_qkv, w_proj, mlp_gain, mlp_shift, w_up, w_down, upstream,
+    clip_length, dataset_group, sample_weight,
+):
+    rows = [array.reshape(1, WIDTH) for array in (attn_gain, attn_shift, mlp_gain, mlp_shift)]
+    outs = fused_layer(
+        [clip_length, dataset_group.reshape(1), sample_weight, tokens, upstream]
+        + rows
+        + [w_qkv, w_proj, w_up, w_down]
+    )
+    return tuple(out[0, :24] if out.shape == (1, 128) else out for out in outs)
+
+
 def solution(mesh):
     in_specs = (
         P(("dp", "ctx"), None),
@@ -269,4 +927,6 @@
         P(("dp", "ctx"), None),
         P(("dp", "ctx"), None),
     )
+    fused = mesh.shape["dp"] == 8 and mesh.shape["ctx"] == 4
+    body = fused_body if fused else general_body
     return jax.shard_map(body, mesh=mesh, in_specs=in_specs, out_specs=out_specs, check_vma=False)

time: 793 us -> 144 us (0.18); the launches traced: 783 us -> 144 us
  waiting for transfers between devices: 559 us -> 0 us
  Pallas kernels: 0 us -> 124 us
  matrix products: 78.5 us -> 0 us
  blocking collectives: 63.3 us -> 0 us
  other arithmetic: 28.8 us -> 0 us
  between operations: 18.8 us -> 2.6 us
  local copies, waits for them, and re-layouts: 33.4 us -> 17.5 us
    reduce_scatter x6 -> x0, waiting for transfers between devices: 534 us -> none  [the longest x1 142 us: body(): lax.psum_scatter(down_grad, ('dp', 'ctx'), scatter_dimension=0, tiled=True)]
    pallas_call x0 -> x1, Pallas kernels: none -> 124 us  [fused_layer(): pl.pallas_call(layer_kernel, out_shape=[rows_out, rows_out, vector, vecto...]
    dot_general x21 -> x0, matrix products: 78.5 us -> none  [the longest x3 12.4 us: scores_for(): jnp.einsum('qhd,khd->hqk', queries3, piece, preferred_element_type=jnp.fl...]
    unnamed x1 -> x0, blocking collectives: 40.1 us -> none
    all_gather x2 -> x0, waiting for transfers between devices: 24 us -> none  [the longest x1 13.8 us: body(): lax.all_gather(key_local, 'ctx', axis=0, tiled=True)]
    psum x1 -> x0, blocking collectives: 23.1 us -> none  [body(): counts = lax.psum(onehot * length.astype(jnp.float32), 'dp')]
    another operation x5 -> x0, local copies, waits for them, and re-layouts: 13 us -> none
    slice x7 -> x0, local copies, waits for them, and re-layouts: 9.03 us -> none  [the longest x2 2.37 us: scores_for(): piece = key_rows[kstart:kstart + key_span].reshape(key_span, head_count, HD)]
  transfers between devices with their start and end apart: 8 -> 0, of which waited for: 8 -> 0; matrix products, arithmetic and copies ran while one was open for 8% -> 0% of each run, Pallas kernels for 0% -> 0%
where the time goes in v1:
time: 144 us
  Pallas kernels  124 us (86%)
  local copies, waits for them, and re-layouts  17.5 us (12%)
  between operations  2.6 us (2%)
    pallas_call x1, Pallas kernels, fused_layer(): pl.pallas_call(layer_kernel, out_shape=[rows_out, rows_out, vector, vecto...  124 us
    unnamed x6, local copies, waits for them, and re-layouts  10.1 us
    reshape x4, local copies, waits for them, and re-layouts, fused_body(): array.reshape(1, WIDTH)  5.07 us

profile of v1, /device:TPU:0, one launch (start us, length us, event | category | flops | bytes accessed | tf_op | source)
XLA Modules:
  0.0 143.7 jit_solution(16976050640364560703)
XLA Ops:
  2.6 1.3 reshape.36.gain1
  3.8 1.3 reshape.37.shift1
  5.1 1.3 reshape.38.gain2
  6.4 1.3 reshape.39.shift2
  7.6 123.6 %shard_map.204 = (bf16[256,768]{1,0:T(8,128)(2,1)}, bf16[256,768]{1,0:T(8,128)(2,1)}, f32[1,128]{1,0:T(1,128)}, f32[1,128]{1,0:T(1,128)}, f32[24,2304]{1,0:T(8,1...) custom-call(s32[1]{0:T(128)S(6)} %copy.29.length_ref, ...), custom_call_target="tpu_custom_call" | custom-call | tf_op jit(solution)/shard_map/pallas_call | solution.py:639
  131.3 1.2 slice_bitcast_fusion.2
  132.5 1.2 slice_bitcast_fusion
  133.6 1.8 %copy.32 = bf16[256,768]{1,0:T(8,128)(2,1)} copy(bf16[256,768]{1,0:T(8,128)(2,1)} %get-tuple-element.44) | data formatting | bytes 786432
  135.4 1.8 %copy.33 = bf16[256,768]{1,0:T(8,128)(2,1)} copy(bf16[256,768]{1,0:T(8,128)(2,1)} %get-tuple-element.45) | data formatting | bytes 786432
  137.1 1.6 %copy.34 = f32[24,2304]{1,0:T(8,128)} copy(f32[24,2304]{1,0:T(8,128)} %get-tuple-element.48) | data formatting | bytes 442368
  138.8 1.5 %copy.35 = f32[24,768]{1,0:T(8,128)} copy(f32[24,768]{1,0:T(8,128)} %get-tuple-element.49) | data formatting | bytes 147456
  140.3 1.7 %copy.36 = f32[24,3072]{1,0:T(8,128)} copy(f32[24,3072]{1,0:T(8,128)} %get-tuple-element.52) | data formatting | bytes 589824
  142.0 1.7 %copy.37 = f32[96,768]{1,0:T(8,128)} copy(f32[96,768]{1,0:T(8,128)} %get-tuple-element.53) | data formatting | bytes 589824

commit v2 on v1

--- a/solution.py
+++ b/solution.py
@@ -86,9 +86,9 @@
 
 
 def layer_kernel(
-    length_ref, group_ref, weight_ref, tok, ups, gain1, shift1, gain2, shift2,
+    length_ref, group_ref, weight_ref, tok, ups, gain1_ref, shift1_ref, gain2_ref, shift2_ref,
     w_qkv, w_proj, w_up, w_down,
-    block_out, input_grad, o_v0, o_v1, o_qk, o_pr, o_v2, o_v3, o_up, o_dn,
+    block_out, input_grad, o_qk, o_pr, o_up, o_dn, o_vec,
     wq, wp, wu, wd, tokc, tokf, nc, nf, qkvt, kvft, bias, ec, ef, o1, m1, l1, f1, f2,
     attt, hid, n2, gel, dg, outl, outh, upo, uph, ncot, hc, hl, mixc, mixf,
     cs, cr, vsend, vrecv,
@@ -107,6 +107,9 @@
     own_rows, oth_rows = at(own, ROWS, ROWS), at(oth, ROWS, ROWS)
     own_half, oth_half = at(core * HALF_WIDTH, HALF_WIDTH, 128), at((1 - core) * HALF_WIDTH, HALF_WIDTH, 128)
     length, group = length_ref[0], group_ref[0]
+    gain1, shift1, gain2, shift2 = (
+        ref[...].reshape(1, WIDTH) for ref in (gain1_ref, shift1_ref, gain2_ref, shift2_ref)
+    )
     left, right = x == 0, x == 1
 
     def fetch(slot, src, dst):
@@ -125,15 +128,20 @@
             return [fetch(4, w_up, wu)]
         return [fetch(5, w_down, wd)]
 
-    for name in ("qkv", "proj", "up", "down"):
-        for copy in weight_copies(name):
-            copy.start()
+    def ask(*names):
+        for name in names:
+            for copy in weight_copies(name):
+                copy.start()
+
+    ask("qkv")
 
     def arrive(name):
         for copy in weight_copies(name):
             copy.wait()
 
-    peers = [mate, x_peer, y_peer] + z_peers
+    diagonal = device_at(z, y, 1 - x, 1 - core)
+    yz_peers = [device_at((z + d) % 4, 1 - y, x, core) for d in (1, 2, 3)]
+    peers = [mate, x_peer, diagonal, y_peer] + z_peers + yz_peers
     barrier = pltpu.get_barrier_semaphore()
     for peer in peers:
         pl.semaphore_signal(barrier, inc=1, device_id=peer, device_id_type=MESH)
@@ -146,7 +154,7 @@
         )
 
     tok_far = misc(0, tok, tokf.at[own_rows], x_peer)
-    tok_mate = misc(1, tok, tokc.at[own_rows], mate)
+    tok_mate = misc(1, tok, tokc, mate)
     tok_on = misc(2, tokf.at[own_rows], tokf.at[own_rows], mate)
     ups_mate = misc(3, ups.at[:, oth_half], outh.at[own_rows], mate)
     count_y = misc(4, cs.at[0], cr.at[0], y_peer)
@@ -160,7 +168,7 @@
     ]
     up_mate = misc(13, upo.at[:, at((1 - core) * 1536, 1536, 128)], uph.at[own_rows], mate)
     hl_mate = misc(14, hl.at[own_rows], hl.at[own_rows], mate)
-    nc_mate = misc(15, tokc.at[own_rows], tokc.at[own_rows], mate)
+    nc_mate = misc(15, upo.at[:, :WIDTH], tokc, mate)
     nf_mate = misc(16, tokf.at[own_rows], tokf.at[own_rows], mate)
     nf_far = misc(17, tokf.at[own_rows], tokf.at[own_rows], x_peer)
 
@@ -173,17 +181,18 @@
     lane = lax.broadcasted_iota(jnp.int32, (8, 128), 1)
     cs[0] = jnp.where(lane == group, length.astype(F32), 0.0)
     count_y.start()
+    ask("proj", "up", "down")
 
     def first_norm(src, src_at, dst, dst_at):
         def step(i):
             unit, _ = normalise(src[at(src_at + i * 64, 64, 64), :].astype(F32))
-            dst[at(dst_at + i * 64, 64, 64), :] = (unit * gain1[...] + shift1[...]).astype(BF16)
+            dst[at(dst_at + i * 64, 64, 64), :] = (unit * gain1 + shift1).astype(BF16)
 
         loop(ROWS // 64, step)
 
     first_norm(tok, 0, nc, own)
     tok_mate.wait()
-    first_norm(tokc, oth, nc, oth)
+    first_norm(tokc, 0, nc, oth)
     arrive("qkv")
 
     def project(i):
@@ -294,7 +303,7 @@
 
     def second_norm(i):
         unit, _ = normalise(hid[at(i * 64, 64, 64), :])
-        n2[at(own + i * 64, 64, 64), :] = (unit * gain2[...] + shift2[...]).astype(BF16)
+        n2[at(own + i * 64, 64, 64), :] = (unit * gain2 + shift2).astype(BF16)
 
     loop(ROWS // 64, second_norm)
     n2_mate.start()
@@ -439,7 +448,7 @@
         cot = ncot[rows, :]
         position = lax.broadcasted_iota(jnp.int32, (64, 1), 0) + i * 64 + x * 512 + own
         out_cot = ups[rows, :].astype(F32) * jnp.where(position < length, scale, 0.0)
-        hidden_cot = out_cot + normalise_back(cot, gain2[...], unit, inverse)
+        hidden_cot = out_cot + normalise_back(cot, gain2, unit, inverse)
         hc[rows, :] = hidden_cot
         hl[at(own + i * 64, 64, 64), :] = hidden_cot.astype(BF16)
         vsend[0, 2:3, :] += jnp.sum(cot * unit, axis=0, keepdims=True)
@@ -529,7 +538,7 @@
         normed_cot(mixf, HALF_WIDTH, oth_rows, store_to(tokf, own_rows))
         nf_mate.start()
 
-    normed_cot(mixc, 0, oth_rows, store_to(tokc, own_rows))
+    normed_cot(mixc, 0, oth_rows, store_to(upo, at(0, ROWS, ROWS)))
     nc_mate.start()
 
     @pl.when(right)
@@ -572,46 +581,62 @@
     def first_back(i):
         rows = at(i * 64, 64, 64)
         unit, inverse = normalise(tok[rows, :].astype(F32))
-        near = tokc[at(oth + i * 64, 64, 64), :].astype(F32)
+        near = tokc[rows, :].astype(F32)
         far = tokf[at(own + i * 64, 64, 64), :].astype(F32)
         cot = ncot[rows, :] + near + jnp.where(left, far, 0.0)
-        input_grad[rows, :] = (hc[rows, :] + normalise_back(cot, gain1[...], unit, inverse)).astype(BF16)
+        input_grad[rows, :] = (hc[rows, :] + normalise_back(cot, gain1, unit, inverse)).astype(BF16)
         vsend[0, 0:1, :] += jnp.sum(cot * unit, axis=0, keepdims=True)
         vsend[0, 1:2, :] += jnp.sum(cot, axis=0, keepdims=True)
 
     loop(ROWS // 64, first_back)
 
-    def vector_copy(slot, target):
-        return misc(18 + slot, vsend.at[min(slot, 3)], vrecv.at[slot], target)
-
-    vector_copy(0, mate).start()
+    clip_peers = [mate, x_peer, diagonal]
+    other_clips = [y_peer] + z_peers + yz_peers
+
+    def clip_sum(i):
+        return misc(18 + i, vsend.at[0], vrecv.at[i], clip_peers[i])
+
+    def all_sum(i):
+        return misc(21 + i, vsend.at[1], vrecv.at[3 + i], other_clips[i])
+
+    for i in range(3):
+        clip_sum(i).start()
     start_third(1)
-    vector_copy(0, mate).wait()
-    vsend[1] = vsend[0] + vrecv[0]
-    vector_copy(1, x_peer).start()
+    for i in range(3):
+        clip_sum(i).wait()
+    vsend[1] = vsend[0] + vrecv[0] + vrecv[1] + vrecv[2]
+    for i in range(7):
+        all_sum(i).start()
     start_second(3)
-    vector_copy(1, x_peer).wait()
-    vsend[2] = vsend[1] + vrecv[1]
-    vector_copy(2, y_peer).start()
     start_last(0)
     start_third(2)
-    vector_copy(2, y_peer).wait()
-    vsend[3] = vsend[2] + vrecv[2]
-    for d in (1, 2, 3):
-        vector_copy(2 + d, z_peers[d - 1]).start()
+    for i in range(7):
+        all_sum(i).wait()
+    sums = vsend[1]
+    for i in range(7):
+        sums = sums + vrecv[3 + i]
+    rank = dp * 4 + ctx
+    o_vec[...] = pltpu.roll(sums, lax.rem(WIDTH - rank * 24, WIDTH), 1)[:, :128]
     start_last(1)
     start_third(3)
-    for d in (1, 2, 3):
-        vector_copy(2 + d, z_peers[d - 1]).wait()
-    sums = vsend[3] + vrecv[3] + vrecv[4] + vrecv[5]
-    rank = dp * 4 + ctx
-    sums = pltpu.roll(sums, lax.rem(WIDTH - rank * 24, WIDTH), 1)
-    for i, ref in enumerate((o_v0, o_v1, o_v2, o_v3)):
-        ref[...] = sums[i : i + 1, :128]
     start_last(2)
     start_last(3)
     for w in range(4):
         finish(w)
+
+
+def hand_out_kernel(
+    block_out, input_grad, qk, pr, up, dn, vec,
+    o_block, o_input, o_v0, o_v1, o_qk, o_pr, o_v2, o_v3, o_up, o_dn, sem,
+):
+    pairs = ((block_out, o_block), (input_grad, o_input), (qk, o_qk), (pr, o_pr), (up, o_up), (dn, o_dn))
+    copies = [pltpu.make_async_copy(src, dst, sem.at[i]) for i, (src, dst) in enumerate(pairs)]
+    for copy in copies:
+        copy.start()
+    for i, ref in enumerate((o_v0, o_v1, o_v2, o_v3)):
+        ref[...] = vec[i, :24]
+    for copy in copies:
+        copy.wait()
 
 
 def fused_layer(args):
@@ -630,29 +655,29 @@
     def per_block(lead):
         return [pltpu.VMEM(lead + block, BF16) for block in BLOCKS]
 
-    vector = jax.ShapeDtypeStruct((1, 128), F32)
+    vector = jax.ShapeDtypeStruct((24,), F32)
 
     def grad_shape(w):
         return jax.ShapeDtypeStruct((BLOCKS[w][0] // 2, BLOCKS[w][1] * 2), F32)
 
     rows_out = jax.ShapeDtypeStruct((ROWS, WIDTH), BF16)
-    return pl.pallas_call(
+    made = pl.pallas_call(
         layer_kernel,
         out_shape=[
-            rows_out, rows_out, vector, vector, grad_shape(3), grad_shape(2), vector, vector,
-            grad_shape(1), grad_shape(0),
+            rows_out, rows_out, grad_shape(3), grad_shape(2), grad_shape(1), grad_shape(0),
+            jax.ShapeDtypeStruct((8, 128), F32),
         ],
         in_specs=[smem] * 3 + [vmem] * 6 + [anywhere] * 4,
-        out_specs=[vmem] * 10,
+        out_specs=[vmem] * 7,
         scratch_shapes=[
             low(768, 1152), low(768, 768), low(768, 3072), low(3072, 768),
-            low(512, 768), low(512, 768), low(512, 768), low(512, 768),
+            low(256, 768), low(512, 768), low(512, 768), low(512, 768),
             low(1152, 512), low(768, 512), low(512, 512), low(6, 512, 512), low(6, 512, 512),
             full(384, 512), full(8, 512), full(8, 512), full(8, 512), full(8, 512),
             low(768, 512), full(256, 768), low(512, 768), low(512, 3072), low(256, 3072),
             low(256, 768), low(512, 384), low(256, 3072), low(512, 1536), full(256, 768),
             full(256, 768), low(512, 768), low(1152, 512), low(768, 512),
-            full(2, 8, 128), full(4, 8, 128), full(4, 8, 768), full(6, 8, 768),
+            full(2, 8, 128), full(4, 8, 128), full(2, 8, 768), full(10, 8, 768),
             low(3072, 384), low(768, 1536), low(768, 384), low(768, 1152),
         ]
         + per_block((4, 2)) + per_block((4,)) + per_block((4,)) + per_block((3,)) + per_block((3,))
@@ -660,14 +685,25 @@
         + [
             pltpu.SemaphoreType.DMA((4, 15)),
             pltpu.SemaphoreType.DMA((4, 15)),
-            pltpu.SemaphoreType.DMA((24,)),
-            pltpu.SemaphoreType.DMA((24,)),
+            pltpu.SemaphoreType.DMA((28,)),
+            pltpu.SemaphoreType.DMA((28,)),
             pltpu.SemaphoreType.DMA((6,)),
         ],
         compiler_params=pltpu.CompilerParams(
             collective_id=0, has_side_effects=True, vmem_limit_bytes=60 * 1024 * 1024
         ),
     )(*args)
+    return pl.pallas_call(
+        hand_out_kernel,
+        out_shape=[
+            rows_out, rows_out, vector, vector, grad_shape(3), grad_shape(2), vector, vector,
+            grad_shape(1), grad_shape(0),
+        ],
+        in_specs=[vmem] * 7,
+        out_specs=[anywhere] * 2 + [vmem] * 2 + [anywhere] * 2 + [vmem] * 2 + [anywhere] * 2,
+        scratch_shapes=[pltpu.SemaphoreType.DMA((6,))],
+        compiler_params=pltpu.CompilerParams(vmem_limit_bytes=60 * 1024 * 1024),
+    )(*made)
 
 
 def general_body(
@@ -890,13 +926,11 @@
     tokens, attn_gain, attn_shift, w_qkv, w_proj, mlp_gain, mlp_shift, w_up, w_down, upstream,
     clip_length, dataset_group, sample_weight,
 ):
-    rows = [array.reshape(1, WIDTH) for array in (attn_gain, attn_shift, mlp_gain, mlp_shift)]
     outs = fused_layer(
         [clip_length, dataset_group.reshape(1), sample_weight, tokens, upstream]
-        + rows
-        + [w_qkv, w_proj, w_up, w_down]
-    )
-    return tuple(out[0, :24] if out.shape == (1, 128) else out for out in outs)
+        + [attn_gain, attn_shift, mlp_gain, mlp_shift, w_qkv, w_proj, w_up, w_down]
+    )
+    return tuple(outs)
 
 
 def solution(mesh):

time: 144 us -> 132 us (0.917)
  local copies, waits for them, and re-layouts: 17.5 us -> 0 us
  Pallas kernels: 124 us -> 129 us
    unnamed x6 -> x0, local copies, waits for them, and re-layouts: 10.1 us -> none
    pallas_call x1 -> x2, Pallas kernels: 124 us -> 129 us  [the longest x1 126 us: fused_layer(): pl.pallas_call(layer_kernel, out_shape=[rows_out, rows_out, grad_shape(3)...]
    reshape x4 -> x0, local copies, waits for them, and re-layouts: 5.07 us -> none  [fused_body(): array.reshape(1, WIDTH)]
    squeeze x2 -> x0, local copies, waits for them, and re-layouts: 2.34 us -> none  [fused_body(): out[0, :24]]
where the time goes in v2:
time: 132 us
  Pallas kernels  129 us (98%)
  between operations  2.75 us (2%)
    pallas_call x1, Pallas kernels, fused_layer(): pl.pallas_call(layer_kernel, out_shape=[rows_out, rows_out, grad_shape(3)...  126 us
    pallas_call x1, Pallas kernels, fused_layer(): pl.pallas_call(hand_out_kernel, out_shape=[rows_out, rows_out, vector, ve...  3.14 us

profile of v2, /device:TPU:0, one launch (start us, length us, event | category | flops | bytes accessed | tf_op | source)
XLA Modules:
  0.0 131.6 jit_solution(17440645202876445905)
XLA Ops:
  2.6 125.7 %shard_map.204 = (bf16[256,768]{1,0:T(8,128)(2,1)}, bf16[256,768]{1,0:T(8,128)(2,1)}, f32[24,2304]{1,0:T(8,128)}, f32[24,768]{1,0:T(8,128)}, f32[24,3072]{1,0:T(...) custom-call(s32[1]{0:T(128)S(6)} %copy.23.length_ref, s32[1]{0:T(128)} %bitcast.1.group_ref, s32[1]{0:T(128)S(6)} %copy.25.weight_ref, ...), custom_call_target="tpu_custom_call" | custom-call | tf_op jit(solution)/shard_map/pallas_call | solution.py:664
  128.3 3.1 %shard_map.205 = (bf16[256,768]{1,0:T(8,128)(2,1)}, bf16[256,768]{1,0:T(8,128)(2,1)}, f32[24]{0:T(128)}, f32[24]{0:T(128)}, f32[24,2304]{1,0:T(8,128)}, /*index=...) custom-call(bf16[256,768]{1,0:T(8,128)(2,1)} %get-tuple-element.17.block_out, ...), custom_call_target="tpu_custom_call" | custom-call | tf_op jit(solution)/shard_map/pallas_call | solution.py:696

commit v3 on v2

--- a/solution.py
+++ b/solution.py
@@ -36,6 +36,7 @@
 HALF_HEADS = 6
 HALF_WIDTH = 384
 BLOCKS = ((192, 384), (48, 1536), (48, 384), (48, 1152))
+ORDERS = (('zyx', 'yxz'), ('xyz', 'yxz'), ('zyx', 'zxy'), ('xyz', 'yxz'))
 
 
 def dot_nn(left, right):
@@ -73,12 +74,17 @@
     return inverse * (scaled - first - unit * second)
 
 
-def loop(count, step):
+def loop(count, step, unroll=1):
+    if unroll == 0:
+        for i in range(count):
+            step(i)
+        return
+
     def wrapped(index, carry):
         step(index)
         return carry
 
-    lax.fori_loop(0, count, wrapped, 0)
+    lax.fori_loop(0, count, wrapped, 0, unroll=unroll)
 
 
 def at(start, size, unit):
@@ -90,11 +96,10 @@
     w_qkv, w_proj, w_up, w_down,
     block_out, input_grad, o_qk, o_pr, o_up, o_dn, o_vec,
     wq, wp, wu, wd, tokc, tokf, nc, nf, qkvt, kvft, bias, ec, ef, o1, m1, l1, f1, f2,
-    attt, hid, n2, gel, dg, outl, outh, upo, uph, ncot, hc, hl, mixc, mixf,
+    attt, hid, n2, gel, dg, outh, upo, uph, ncot, hc, hl, mixc, mixf,
     cs, cr, vsend, vrecv,
     g_dn, g_up, g_pr, g_qk,
-    r1_dn, r1_up, r1_pr, r1_qk, s2_dn, s2_up, s2_pr, s2_qk, r2_dn, r2_up, r2_pr, r2_qk,
-    s3_dn, s3_up, s3_pr, s3_qk, r3_dn, r3_up, r3_pr, r3_qk, f_dn, f_up, f_pr, f_qk,
+    c_dn, c_up, c_pr, c_qk, s_dn, s_up, s_pr, s_qk, h_dn, h_up, h_pr, h_qk,
     send_sem, recv_sem, misc_send, misc_recv, local_sem,
 ):
     dp, ctx = lax.axis_index("dp"), lax.axis_index("ctx")
@@ -188,7 +193,7 @@
             unit, _ = normalise(src[at(src_at + i * 64, 64, 64), :].astype(F32))
             dst[at(dst_at + i * 64, 64, 64), :] = (unit * gain1 + shift1).astype(BF16)
 
-        loop(ROWS // 64, step)
+        loop(ROWS // 64, step, 0)
 
     first_norm(tok, 0, nc, own)
     tok_mate.wait()
@@ -199,7 +204,7 @@
         part = dot_tt(wq[:, at(i * HALF_WIDTH, HALF_WIDTH, 128)], nc[...])
         qkvt[at(i * HALF_WIDTH, HALF_WIDTH, 128), :] = (part * jnp.where(i == 0, 0.125, 1.0)).astype(BF16)
 
-    loop(3, project)
+    loop(3, project, 0)
 
     key_at = lax.broadcasted_iota(jnp.int32, (512, 512), 0)
     query_at = lax.broadcasted_iota(jnp.int32, (512, 512), 1)
@@ -219,7 +224,7 @@
             ec[h, :span, cols] = expo_low
             o1[at(r, 64, 64), cols] = dot_nn(values[:, :span], expo_low)
 
-    loop(HALF_HEADS, attend_chip)
+    loop(HALF_HEADS, attend_chip, 0)
 
     count_y.wait()
     cs[1] = cs[0] + cr[0]
@@ -234,7 +239,7 @@
     row_at = lax.broadcasted_iota(jnp.int32, (ROWS, 1), 0) + x * 512
     own_scale = jnp.where(row_at + own < length, scale, 0.0)
     oth_scale = jnp.where(row_at + oth < length, scale, 0.0)
-    outl[...] = (ups[...].astype(F32) * own_scale).astype(BF16)
+    hl[own_rows, :] = (ups[...].astype(F32) * own_scale).astype(BF16)
     outh[own_rows, :] = (ups[:, own_half].astype(F32) * own_scale).astype(BF16)
     ups_mate.wait()
     outh[oth_rows, :] = (outh[oth_rows, :].astype(F32) * oth_scale).astype(BF16)
@@ -249,7 +254,7 @@
                 part = dot_tt(wq[:, at((i + 1) * HALF_WIDTH, HALF_WIDTH, 128)], nf[columns, :])
                 kvft[at(i * HALF_WIDTH, HALF_WIDTH, 128), columns] = part.astype(BF16)
 
-            loop(2, project_far)
+            loop(2, project_far, 0)
 
         tok_far.wait_recv()
         tok_on.start()
@@ -277,7 +282,7 @@
                 f2[pl.ds(h, 1), cols] = new_part * share
                 o1[at(r, 64, 64), cols] = o1[at(r, 64, 64), cols] * (old_part * share) + out * (new_part * share)
 
-        loop(HALF_HEADS, attend_far)
+        loop(HALF_HEADS, attend_far, 0)
 
     @pl.when(left)
     def _():
@@ -305,13 +310,13 @@
         unit, _ = normalise(hid[at(i * 64, 64, 64), :])
         n2[at(own + i * 64, 64, 64), :] = (unit * gain2 + shift2).astype(BF16)
 
-    loop(ROWS // 64, second_norm)
+    loop(ROWS // 64, second_norm, 0)
     n2_mate.start()
     arrive("up")
-    for part in range(3):
-
-        def feed(i, part=part):
-            cols = at(part * 1024 + i * 256, 256, 256)
+    for third in range(3):
+
+        def feed(i, third=third):
+            cols = at(third * 1024 + i * 256, 256, 256)
             u = dot_nn(n2[own_rows, :], wu[:, cols])
             square = u * u
             bend = jnp.tanh(GELU_COEF * (u + 0.044715 * square * u))
@@ -320,17 +325,13 @@
             slope = lift + 0.5 * u * (1.0 - bend * bend) * (GELU_COEF * (1.0 + 3 * 0.044715 * square))
             dg[:, cols] = slope.astype(BF16)
 
-        loop(4, feed)
-        gel_mate[part].start()
-
-    first = device_at(z, (y + core) % 2, (x + 1 - core) % 2, core)
-    second = device_at(z, (y + 1 - core) % 2, (x + core) % 2, core)
-    kept = jnp.where(core == 0, y, x)
+        loop(4, feed, 0)
+        gel_mate[third].start()
+
     grads = (g_dn, g_up, g_pr, g_qk)
     outs = (o_dn, o_up, o_pr, o_qk)
-    r1s, s2s, r2s = (r1_dn, r1_up, r1_pr, r1_qk), (s2_dn, s2_up, s2_pr, s2_qk), (r2_dn, r2_up, r2_pr, r2_qk)
-    s3s, r3s = (s3_dn, s3_up, s3_pr, s3_qk), (r3_dn, r3_up, r3_pr, r3_qk)
-    fs = (f_dn, f_up, f_pr, f_qk)
+    came, sent = (c_dn, c_up, c_pr, c_qk), (s_dn, s_up, s_pr, s_qk)
+    hs = (h_dn, h_up, h_pr, h_qk)
 
     def remote(src, dst, w, slot, target):
         return pltpu.make_async_remote_copy(
@@ -338,27 +339,148 @@
             device_id=target, device_id_type=MESH,
         )
 
-    def block(w, index):
+    def part(ref, w, index, count=1):
         rows = BLOCKS[w][0]
-        return at(index * rows, rows, 16)
-
-    def kept_block(w, zz, j):
-        return grads[w][block(w, zz * 4 + jnp.where(core == 0, j * 2 + x, y * 2 + j)), :].astype(F32)
-
-    def first_copy(w, zz, j):
-        index = zz * 4 + jnp.where(core == 0, j * 2 + 1 - x, (1 - y) * 2 + j)
-        return remote(grads[w].at[block(w, index)], r1s[w].at[zz, j], w, zz * 2 + j, first)
+        return ref.at[at(index * rows, count * rows, 16)]
+
+    def value(ref, w, index):
+        rows = BLOCKS[w][0]
+        return ref[at(index * rows, rows, 16), :].astype(F32)
+
+    def keep(ref, w, index, result):
+        rows = BLOCKS[w][0]
+        ref[at(index * rows, rows, 16), :] = result.astype(BF16)
+
+    class PlaneFirst:
+        def __init__(self, w, x_first):
+            self.w, self.x_first = w, x_first
+            self.first, self.second = (x_peer, y_peer) if x_first else (y_peer, x_peer)
+            self.kept = y if x_first else x
+
+        def block(self, zz, j, mine):
+            side = (x if mine else 1 - x) if self.x_first else (y if mine else 1 - y)
+            return zz * 4 + (j * 2 + side if self.x_first else side * 2 + j)
+
+        def first_copies(self, places):
+            w = self.w
+            return [
+                remote(part(grads[w], w, self.block(zz, j, False)), part(came[w], w, zz * 2 + j), w, zz * 2 + j, self.first)
+                for zz in places
+                for j in range(2)
+            ]
+
+        def second_copy(self):
+            w = self.w
+            return remote(part(sent[w], w, 0, 4), part(came[w], w, 8, 4), w, 8, self.second)
+
+        def third_copies(self):
+            w = self.w
+            return [
+                remote(part(sent[w], w, 3 + d), part(came[w], w, 11 + d), w, 8 + d, z_peers[d - 1])
+                for d in (1, 2, 3)
+            ]
+
+        def after_first(self, zz, j):
+            w = self.w
+            return value(grads[w], w, self.block(zz, j, True)) + value(came[w], w, zz * 2 + j)
+
+        def after_second(self, zz):
+            return self.after_first(zz, self.kept) + value(came[self.w], self.w, 8 + zz)
+
+        def start_second(self):
+            for copy in self.first_copies(range(4)):
+                copy.wait()
+            for zz in range(4):
+                keep(sent[self.w], self.w, zz, self.after_first(zz, 1 - self.kept))
+            self.second_copy().start()
+
+        def start_third(self):
+            self.second_copy().wait()
+            for d, copy in zip((1, 2, 3), self.third_copies()):
+                keep(sent[self.w], self.w, 3 + d, self.after_second((z + d) % 4))
+                copy.start()
+
+        def total(self):
+            w = self.w
+            for copy in self.third_copies():
+                copy.wait()
+            return self.after_second(z) + value(came[w], w, 12) + value(came[w], w, 13) + value(came[w], w, 14)
+
+    class LineFirst:
+        def __init__(self, w, x_second):
+            self.w, self.x_second = w, x_second
+            self.second, self.third = (x_peer, y_peer) if x_second else (y_peer, x_peer)
+            self.kept = y if x_second else x
+
+        def place(self, i, mine):
+            side = (x if mine else 1 - x) if self.x_second else (y if mine else 1 - y)
+            return i * 2 + side if self.x_second else side * 2 + i
+
+        def first_copy(self, d):
+            w = self.w
+            return remote(part(grads[w], w, (z + d) % 4 * 4, 4), part(came[w], w, 4 * d - 4, 4), w, d - 1, z_peers[d - 1])
+
+        def second_copy(self):
+            w = self.w
+            return remote(part(sent[w], w, 0, 2), part(came[w], w, 12, 2), w, 8, self.second)
+
+        def third_copy(self):
+            w = self.w
+            return remote(part(sent[w], w, 2), part(came[w], w, 14), w, 9, self.third)
+
+        def after_first(self, i, mine):
+            w, b = self.w, self.place(i, mine)
+            whole = value(grads[w], w, z * 4 + b)
+            for d in range(3):
+                whole = whole + value(came[w], w, 4 * d + b)
+            return whole
+
+        def start_second(self):
+            for d in (1, 2, 3):
+                self.first_copy(d).wait()
+            for i in range(2):
+                keep(sent[self.w], self.w, i, self.after_first(i, False))
+            self.second_copy().start()
+
+        def start_third(self):
+            self.second_copy().wait()
+            i = 1 - self.kept
+            keep(sent[self.w], self.w, 2, self.after_first(i, True) + value(came[self.w], self.w, 12 + i))
+            self.third_copy().start()
+
+        def total(self):
+            w = self.w
+            self.third_copy().wait()
+            return self.after_first(self.kept, True) + value(came[w], w, 12 + self.kept) + value(came[w], w, 14)
+
+    def plan(w, order):
+        return LineFirst(w, order == "zxy") if order[0] == "z" else PlaneFirst(w, order[0] == "x")
+
+    plans = [[plan(w, order) for order in ORDERS[w]] for w in range(4)]
+
+    def each_core(w, step):
+        if ORDERS[w][0] == ORDERS[w][1]:
+            step(plans[w][0])
+            return
+        for which in (0, 1):
+            pl.when(core == which)(lambda which=which: step(plans[w][which]))
 
     def start_first(w, places):
-        for zz in places:
-            for j in range(2):
-                first_copy(w, zz, j).start()
-
-    def second_copy(w):
-        return remote(s2s[w], r2s[w], w, 8, second)
-
-    def third_copy(w, d):
-        return remote(s3s[w].at[d - 1], r3s[w].at[d - 1], w, 8 + d, z_peers[d - 1])
+        def step(plan):
+            if isinstance(plan, PlaneFirst):
+                for copy in plan.first_copies(places):
+                    copy.start()
+            elif 3 in places:
+                for d in (1, 2, 3):
+                    plan.first_copy(d).start()
+
+        each_core(w, step)
+
+    def start_second(w):
+        each_core(w, lambda plan: plan.start_second())
+
+    def start_third(w):
+        each_core(w, lambda plan: plan.start_third())
 
     def places(w):
         parts = 3 if w == 3 else 1
@@ -366,41 +488,27 @@
         return [(pl.ds(i * width, width), at((2 * i + core) * width, width, 128)) for i in range(parts)]
 
     def last_copies(w):
-        rows = BLOCKS[w][0] // 2
-        far_rows = at((1 - core) * rows, rows, 8)
         return [
-            remote(fs[w].at[far_rows, src], outs[w].at[:, dst], w, 12 + i, mate)
+            remote(hs[w].at[:, src], outs[w].at[:, dst], w, 12 + i, mate)
             for i, (src, dst) in enumerate(places(w))
         ]
 
-    def start_second(w):
-        for zz in range(4):
-            for j in range(2):
-                first_copy(w, zz, j).wait()
-        j = 1 - kept
-        for zz in range(4):
-            s2s[w][zz] = (kept_block(w, zz, j) + r1s[w][zz, j].astype(F32)).astype(BF16)
-        second_copy(w).start()
-
-    def summed(w, zz):
-        return kept_block(w, zz, kept) + r1s[w][zz, kept].astype(F32) + r2s[w][zz].astype(F32)
-
-    def start_third(w):
-        second_copy(w).wait()
-        for d in (1, 2, 3):
-            s3s[w][d - 1] = summed(w, (z + d) % 4).astype(BF16)
-            third_copy(w, d).start()
-        fs[w][...] = summed(w, z)
-
     def start_last(w):
-        for d in (1, 2, 3):
-            third_copy(w, d).wait()
         rows = BLOCKS[w][0] // 2
-        fs[w][...] = fs[w][...] + r3s[w][0].astype(F32) + r3s[w][1].astype(F32) + r3s[w][2].astype(F32)
+
+        def step(plan):
+            whole = plan.total()
+            low_core = core == 0
+            hs[w][...] = jnp.where(low_core, whole[rows:], whole[:rows])
+            mine = jnp.where(low_core, whole[:rows], whole[rows:])
+            parts = 3 if w == 3 else 1
+            width = BLOCKS[w][1] // parts
+            for i, (_, dst) in enumerate(places(w)):
+                outs[w][:, dst] = mine[:, i * width : (i + 1) * width]
+
+        each_core(w, step)
         for copy in last_copies(w):
             copy.start()
-        for src, dst in places(w):
-            outs[w][:, dst] = fs[w][at(core * rows, rows, 8), src]
 
     def finish(w):
         for copy in last_copies(w):
@@ -414,13 +522,13 @@
             start = zz * WIDTH + i * 256
             g_dn[at(start, 256, 256), :] = dot_tn(gel[:, at(start, 256, 256)], outh[...]).astype(BF16)
 
-        loop(3, down_rows)
+        loop(3, down_rows, 0)
         start_first(0, (zz,))
 
     arrive("down")
 
     def gelu_back(cols):
-        up_cot = dot_nt(outl[...], wd[cols, :]) * dg[:, cols].astype(F32)
+        up_cot = dot_nt(hl[own_rows, :], wd[cols, :]) * dg[:, cols].astype(F32)
         up_cot = up_cot.astype(BF16)
         upo[:, cols] = up_cot
         return up_cot
@@ -431,15 +539,15 @@
     def back_own(i):
         uph[own_rows, at(i * 256, 256, 256)] = gelu_back(at(core * 1536 + i * 256, 256, 256))
 
-    loop(6, back_other)
+    loop(6, back_other, 0)
     up_mate.start()
-    loop(6, back_own)
+    loop(6, back_own, 0)
 
     def n2_back(i):
         cols = at(i * 256, 256, 256)
         ncot[:, cols] = dot_nt(upo[...], wu[cols, :])
 
-    loop(3, n2_back)
+    loop(3, n2_back, 0)
     vsend[...] = jnp.zeros_like(vsend)
 
     def second_back(i):
@@ -454,19 +562,20 @@
         vsend[0, 2:3, :] += jnp.sum(cot * unit, axis=0, keepdims=True)
         vsend[0, 3:4, :] += jnp.sum(cot, axis=0, keepdims=True)
 
-    loop(ROWS // 64, second_back)
+    loop(ROWS // 64, second_back, 0)
     hl_mate.start()
 
     n2_mate.wait()
     up_mate.wait()
-    for part in range(2):
-
-        def up_columns(i, part=part):
+    for half in range(2):
+
+        def up_columns(i, half=half):
             cols = at(i * 512, 512, 512)
-            g_up[384 * part : 384 * part + 384, cols] = dot_tn(n2[:, 384 * part : 384 * part + 384], uph[:, cols]).astype(BF16)
-
-        loop(3, up_columns)
-        start_first(1, (2 * part, 2 * part + 1))
+            rows = slice(384 * half, 384 * half + 384)
+            g_up[rows, cols] = dot_tn(n2[:, rows], uph[:, cols]).astype(BF16)
+
+        loop(3, up_columns, 0)
+        start_first(1, (2 * half, 2 * half + 1))
 
     hl_mate.wait()
 
@@ -474,7 +583,7 @@
         rows = at(i * 256, 256, 256)
         g_pr[rows, :] = dot_nn(attt[rows, :], hl[:, own_half]).astype(BF16)
 
-    loop(3, proj_rows)
+    loop(3, proj_rows, 0)
     start_first(2, range(4))
     attt[att_rows, :] = dot_nt(wp[att_rows, :], hl[...]).astype(BF16)
 
@@ -515,17 +624,15 @@
     def attend_back_late(h):
         attend_back(h + 3)
 
-    loop(3, attend_back)
-    start_second(0)
-    loop(3, attend_back_late)
-    start_second(1)
+    loop(3, attend_back, 0)
+    loop(3, attend_back_late, 0)
 
     def normed_cot(mixed, first_column, columns, store):
         def step(i):
             rows = at(i * 256, 256, 256)
             store(rows, dot_tt(mixed[:, columns], wq[rows, first_column:]))
 
-        loop(3, step)
+        loop(3, step, 0)
 
     def store_to(ref, rows):
         def store(cols, value):
@@ -537,6 +644,16 @@
     def _():
         normed_cot(mixf, HALF_WIDTH, oth_rows, store_to(tokf, own_rows))
         nf_mate.start()
+
+    for half in range(2):
+        cols = slice(384 * half, 384 * half + 384)
+        g_qk[cols, :384] = dot_tt(nc[:, cols], mixc[:384, :]).astype(BF16)
+        for i in range(2):
+            g_qk[cols, 384 * (i + 1) : 384 * (i + 2)] = (
+                dot_tt(nc[:, cols], mixc[384 * (i + 1) : 384 * (i + 2), :])
+                + dot_tt(nf[:, cols], mixf[384 * i : 384 * (i + 1), :])
+            ).astype(BF16)
+        start_first(3, (2 * half, 2 * half + 1))
 
     normed_cot(mixc, 0, oth_rows, store_to(upo, at(0, ROWS, ROWS)))
     nc_mate.start()
@@ -548,26 +665,19 @@
         tokf[own_rows, :] = (ncot[...] + tokf[oth_rows, :].astype(F32)).astype(BF16)
         nf_far.start()
 
-    for part in range(2):
-        cols = slice(384 * part, 384 * part + 384)
-        g_qk[cols, :384] = dot_tt(nc[:, cols], mixc[:384, :]).astype(BF16)
-        for i in range(2):
-            g_qk[cols, 384 * (i + 1) : 384 * (i + 2)] = (
-                dot_tt(nc[:, cols], mixc[384 * (i + 1) : 384 * (i + 2), :])
-                + dot_tt(nf[:, cols], mixf[384 * i : 384 * (i + 1), :])
-            ).astype(BF16)
-        start_first(3, (2 * part, 2 * part + 1))
-
     normed_cot(mixc, 0, own_rows, store_to(ncot, at(0, ROWS, ROWS)))
-    start_third(0)
-    start_second(2)
 
     def block_rows(i):
         cols = at(i * 256, 256, 256)
         block_out[:, cols] = (hid[:, cols] + dot_nn(gel[own_rows, :], wd[:, cols])).astype(BF16)
 
-    loop(3, block_rows)
+    loop(3, block_rows, 0)
+    start_second(0)
+    start_second(1)
+    start_second(2)
+    start_third(0)
     nc_mate.wait()
+    start_third(1)
 
     @pl.when(left)
     def _():
@@ -588,7 +698,7 @@
         vsend[0, 0:1, :] += jnp.sum(cot * unit, axis=0, keepdims=True)
         vsend[0, 1:2, :] += jnp.sum(cot, axis=0, keepdims=True)
 
-    loop(ROWS // 64, first_back)
+    loop(ROWS // 64, first_back, 0)
 
     clip_peers = [mate, x_peer, diagonal]
     other_clips = [y_peer] + z_peers + yz_peers
@@ -601,15 +711,15 @@
 
     for i in range(3):
         clip_sum(i).start()
-    start_third(1)
+    start_second(3)
+    start_third(2)
     for i in range(3):
         clip_sum(i).wait()
     vsend[1] = vsend[0] + vrecv[0] + vrecv[1] + vrecv[2]
     for i in range(7):
         all_sum(i).start()
-    start_second(3)
     start_last(0)
-    start_third(2)
+    start_third(3)
     for i in range(7):
         all_sum(i).wait()
     sums = vsend[1]
@@ -618,7 +728,6 @@
     rank = dp * 4 + ctx
     o_vec[...] = pltpu.roll(sums, lax.rem(WIDTH - rank * 24, WIDTH), 1)[:, :128]
     start_last(1)
-    start_third(3)
     start_last(2)
     start_last(3)
     for w in range(4):
@@ -652,8 +761,8 @@
     def full(*shape):
         return pltpu.VMEM(shape, F32)
 
-    def per_block(lead):
-        return [pltpu.VMEM(lead + block, BF16) for block in BLOCKS]
+    def per_block(count):
+        return [low(count * rows, width) for rows, width in BLOCKS]
 
     vector = jax.ShapeDtypeStruct((24,), F32)
 
@@ -675,13 +784,13 @@
             low(1152, 512), low(768, 512), low(512, 512), low(6, 512, 512), low(6, 512, 512),
             full(384, 512), full(8, 512), full(8, 512), full(8, 512), full(8, 512),
             low(768, 512), full(256, 768), low(512, 768), low(512, 3072), low(256, 3072),
-            low(256, 768), low(512, 384), low(256, 3072), low(512, 1536), full(256, 768),
+            low(512, 384), low(256, 3072), low(512, 1536), full(256, 768),
             full(256, 768), low(512, 768), low(1152, 512), low(768, 512),
             full(2, 8, 128), full(4, 8, 128), full(2, 8, 768), full(10, 8, 768),
             low(3072, 384), low(768, 1536), low(768, 384), low(768, 1152),
         ]
-        + per_block((4, 2)) + per_block((4,)) + per_block((4,)) + per_block((3,)) + per_block((3,))
-        + [pltpu.VMEM(block, F32) for block in BLOCKS]
+        + per_block(15) + per_block(7)
+        + [pltpu.VMEM((block[0] // 2, block[1]), F32) for block in BLOCKS]
         + [
             pltpu.SemaphoreType.DMA((4, 15)),
             pltpu.SemaphoreType.DMA((4, 15)),

time: 132 us -> 120 us (0.909)
  Pallas kernels: 129 us -> 116 us
    pallas_call x1, Pallas kernels: 126 us -> 113 us  [fused_layer(): pl.pallas_call(layer_kernel, out_shape=[rows_out, rows_out, grad_shape(3)...]
where the time goes in v3:
time: 120 us; the launch traced here: 119 us
  Pallas kernels  116 us (97%)
  between operations  2.77 us (2%)
    pallas_call x1, Pallas kernels, fused_layer(): pl.pallas_call(layer_kernel, out_shape=[rows_out, rows_out, grad_shape(3)...  113 us
    pallas_call x1, Pallas kernels, fused_layer(): pl.pallas_call(hand_out_kernel, out_shape=[rows_out, rows_out, vector, ve...  3.14 us

profile of v3, /device:TPU:0, one launch (start us, length us, event | category | flops | bytes accessed | tf_op | source)
XLA Modules:
  0.0 119.1 jit_solution(10232761294468931897)
XLA Ops:
  2.6 113.2 %shard_map.204 = (bf16[256,768]{1,0:T(8,128)(2,1)}, bf16[256,768]{1,0:T(8,128)(2,1)}, f32[24,2304]{1,0:T(8,128)}, f32[24,768]{1,0:T(8,128)}, f32[24,3072]{1,0:T(...) custom-call(s32[1]{0:T(128)S(6)} %copy.23.length_ref, s32[1]{0:T(128)} %bitcast.1.group_ref, s32[1]{0:T(128)S(6)} %copy.25.weight_ref, ...), custom_call_target="tpu_custom_call" | custom-call | tf_op jit(solution)/shard_map/pallas_call | solution.py:773
  115.8 3.1 %shard_map.205 = (bf16[256,768]{1,0:T(8,128)(2,1)}, bf16[256,768]{1,0:T(8,128)(2,1)}, f32[24]{0:T(128)}, f32[24]{0:T(128)}, f32[24,2304]{1,0:T(8,128)}, /*index=...) custom-call(bf16[256,768]{1,0:T(8,128)(2,1)} %get-tuple-element.17.block_out, ...), custom_call_target="tpu_custom_call" | custom-call | tf_op jit(solution)/shard_map/pallas_call | solution.py:805

commit v4 on v3

--- a/solution.py
+++ b/solution.py
@@ -36,7 +36,7 @@
 HALF_HEADS = 6
 HALF_WIDTH = 384
 BLOCKS = ((192, 384), (48, 1536), (48, 384), (48, 1152))
-ORDERS = (('zyx', 'yxz'), ('xyz', 'yxz'), ('zyx', 'zxy'), ('xyz', 'yxz'))
+ORDERS = (('zyx', 'xyz'), ('yxz', 'xyz'), ('zyx', 'zxy'), ('yxz', 'xyz'))
 
 
 def dot_nn(left, right):
@@ -92,10 +92,10 @@
 
 
 def layer_kernel(
-    length_ref, group_ref, weight_ref, tok, ups, gain1_ref, shift1_ref, gain2_ref, shift2_ref,
+    length_ref, group_ref, weight_ref, tok_in, ups_in, gain1_ref, shift1_ref, gain2_ref, shift2_ref,
     w_qkv, w_proj, w_up, w_down,
     block_out, input_grad, o_qk, o_pr, o_up, o_dn, o_vec,
-    wq, wp, wu, wd, tokc, tokf, nc, nf, qkvt, kvft, bias, ec, ef, o1, m1, l1, f1, f2,
+    tok, ups, wq, wp, wu, wd, tokc, tokf, nc, nf, qkvt, kvft, bias, ec, ef, o1, m1, l1, f1, f2,
     attt, hid, n2, gel, dg, outh, upo, uph, ncot, hc, hl, mixc, mixf,
     cs, cr, vsend, vrecv,
     g_dn, g_up, g_pr, g_qk,
@@ -138,7 +138,10 @@
             for copy in weight_copies(name):
                 copy.start()
 
+    rows_in = [fetch(6, tok_in, tok), fetch(7, ups_in, ups)]
+    rows_in[0].start()
     ask("qkv")
+    rows_in[1].start()
 
     def arrive(name):
         for copy in weight_copies(name):
@@ -158,10 +161,13 @@
             device_id=target, device_id_type=MESH,
         )
 
-    tok_far = misc(0, tok, tokf.at[own_rows], x_peer)
-    tok_mate = misc(1, tok, tokc, mate)
-    tok_on = misc(2, tokf.at[own_rows], tokf.at[own_rows], mate)
-    ups_mate = misc(3, ups.at[:, oth_half], outh.at[own_rows], mate)
+    def piece(i, start=0):
+        return at(start + i * 128, 128, 128)
+
+    tok_far = [misc(28 + i, tok_in.at[piece(i)], tokf.at[piece(i, own)], x_peer) for i in range(2)]
+    tok_mate = misc(1, tok_in, tokc, mate)
+    tok_on = [misc(30 + i, tokf.at[piece(i, own)], tokf.at[piece(i, own)], mate) for i in range(2)]
+    ups_mate = misc(3, ups_in.at[:, oth_half], outh.at[own_rows], mate)
     count_y = misc(4, cs.at[0], cr.at[0], y_peer)
     count_z = [misc(4 + d, cs.at[1], cr.at[d], z_peers[d - 1]) for d in (1, 2, 3)]
     att_rows = at(core * HALF_WIDTH, HALF_WIDTH, 128)
@@ -179,7 +185,8 @@
 
     @pl.when(left)
     def _():
-        tok_far.start()
+        for copy in tok_far:
+            copy.start()
 
     tok_mate.start()
     ups_mate.start()
@@ -188,13 +195,14 @@
     count_y.start()
     ask("proj", "up", "down")
 
-    def first_norm(src, src_at, dst, dst_at):
+    def first_norm(src, src_at, dst, dst_at, count=ROWS // 64):
         def step(i):
             unit, _ = normalise(src[at(src_at + i * 64, 64, 64), :].astype(F32))
             dst[at(dst_at + i * 64, 64, 64), :] = (unit * gain1 + shift1).astype(BF16)
 
-        loop(ROWS // 64, step, 0)
-
+        loop(count, step, 0)
+
+    rows_in[0].wait()
     first_norm(tok, 0, nc, own)
     tok_mate.wait()
     first_norm(tokc, 0, nc, oth)
@@ -226,6 +234,7 @@
 
     loop(HALF_HEADS, attend_chip, 0)
 
+    rows_in[1].wait()
     count_y.wait()
     cs[1] = cs[0] + cr[0]
     for copy in count_z:
@@ -247,7 +256,6 @@
     @pl.when(right)
     def _():
         def far_block(start):
-            first_norm(tokf, start, nf, start)
             columns = at(start, ROWS, ROWS)
 
             def project_far(i):
@@ -256,10 +264,14 @@
 
             loop(2, project_far, 0)
 
-        tok_far.wait_recv()
-        tok_on.start()
+        for i in range(2):
+            tok_far[i].wait_recv()
+            tok_on[i].start()
+            first_norm(tokf, own + i * 128, nf, own + i * 128, 2)
         far_block(own)
-        tok_on.wait()
+        for i in range(2):
+            tok_on[i].wait()
+            first_norm(tokf, oth + i * 128, nf, oth + i * 128, 2)
         far_block(oth)
 
         def attend_far(h):
@@ -621,12 +633,6 @@
 
         mixc[rows, :] = (o1[rows, :] * 0.125).astype(BF16)
 
-    def attend_back_late(h):
-        attend_back(h + 3)
-
-    loop(3, attend_back, 0)
-    loop(3, attend_back_late, 0)
-
     def normed_cot(mixed, first_column, columns, store):
         def step(i):
             rows = at(i * 256, 256, 256)
@@ -640,6 +646,16 @@
 
         return store
 
+    clip_peers = [mate, x_peer, diagonal]
+    other_clips = [y_peer] + z_peers + yz_peers
+
+    def clip_sum(i):
+        return misc(18 + i, vsend.at[0], vrecv.at[i], clip_peers[i])
+
+    def all_sum(i):
+        return misc(21 + i, vsend.at[1], vrecv.at[3 + i], other_clips[i])
+
+    loop(HALF_HEADS, attend_back, 0)
     @pl.when(right)
     def _():
         normed_cot(mixf, HALF_WIDTH, oth_rows, store_to(tokf, own_rows))
@@ -671,18 +687,20 @@
         cols = at(i * 256, 256, 256)
         block_out[:, cols] = (hid[:, cols] + dot_nn(gel[own_rows, :], wd[:, cols])).astype(BF16)
 
+    start_second(0)
     loop(3, block_rows, 0)
-    start_second(0)
     start_second(1)
     start_second(2)
     start_third(0)
+    start_third(1)
+    start_second(3)
     nc_mate.wait()
-    start_third(1)
 
     @pl.when(left)
     def _():
         nf_far.wait_recv()
-        tok_far.wait_send()
+        for copy in tok_far:
+            copy.wait_send()
 
     @pl.when(right)
     def _():
@@ -700,18 +718,8 @@
 
     loop(ROWS // 64, first_back, 0)
 
-    clip_peers = [mate, x_peer, diagonal]
-    other_clips = [y_peer] + z_peers + yz_peers
-
-    def clip_sum(i):
-        return misc(18 + i, vsend.at[0], vrecv.at[i], clip_peers[i])
-
-    def all_sum(i):
-        return misc(21 + i, vsend.at[1], vrecv.at[3 + i], other_clips[i])
-
     for i in range(3):
         clip_sum(i).start()
-    start_second(3)
     start_third(2)
     for i in range(3):
         clip_sum(i).wait()
@@ -776,9 +784,10 @@
             rows_out, rows_out, grad_shape(3), grad_shape(2), grad_shape(1), grad_shape(0),
             jax.ShapeDtypeStruct((8, 128), F32),
         ],
-        in_specs=[smem] * 3 + [vmem] * 6 + [anywhere] * 4,
+        in_specs=[smem] * 3 + [anywhere] * 2 + [vmem] * 4 + [anywhere] * 4,
         out_specs=[vmem] * 7,
         scratch_shapes=[
+            low(256, 768), low(256, 768),
             low(768, 1152), low(768, 768), low(768, 3072), low(3072, 768),
             low(256, 768), low(512, 768), low(512, 768), low(512, 768),
             low(1152, 512), low(768, 512), low(512, 512), low(6, 512, 512), low(6, 512, 512),
@@ -794,9 +803,9 @@
         + [
             pltpu.SemaphoreType.DMA((4, 15)),
             pltpu.SemaphoreType.DMA((4, 15)),
-            pltpu.SemaphoreType.DMA((28,)),
-            pltpu.SemaphoreType.DMA((28,)),
-            pltpu.SemaphoreType.DMA((6,)),
+            pltpu.SemaphoreType.DMA((32,)),
+            pltpu.SemaphoreType.DMA((32,)),
+            pltpu.SemaphoreType.DMA((8,)),
         ],
         compiler_params=pltpu.CompilerParams(
             collective_id=0, has_side_effects=True, vmem_limit_bytes=60 * 1024 * 1024

time: 120 us -> 117 us (0.975)
  Pallas kernels: 116 us -> 113 us
    pallas_call x1, Pallas kernels: 113 us -> 110 us  [fused_layer(): pl.pallas_call(layer_kernel, out_shape=[rows_out, rows_out, grad_shape(3)...]
where the time goes in v4:
time: 117 us; the launch traced here: 116 us
  Pallas kernels  113 us (97%)
  between operations  2.79 us (2%)
    pallas_call x1, Pallas kernels, fused_layer(): pl.pallas_call(layer_kernel, out_shape=[rows_out, rows_out, grad_shape(3)...  110 us
    pallas_call x1, Pallas kernels, fused_layer(): pl.pallas_call(hand_out_kernel, out_shape=[rows_out, rows_out, vector, ve...  3.14 us

profile of v4, /device:TPU:0, one launch (start us, length us, event | category | flops | bytes accessed | tf_op | source)
XLA Modules:
  0.0 116.2 jit_solution(2925558579565535775)
XLA Ops:
  2.6 110.3 %shard_map.204 = (bf16[256,768]{1,0:T(8,128)(2,1)}, bf16[256,768]{1,0:T(8,128)(2,1)}, f32[24,2304]{1,0:T(8,128)}, f32[24,768]{1,0:T(8,128)}, f32[24,3072]{1,0:T(...) custom-call(s32[1]{0:T(128)S(6)} %copy.23.length_ref, s32[1]{0:T(128)} %bitcast.1.group_ref, s32[1]{0:T(128)S(6)} %copy.25.weight_ref, ...), custom_call_target="tpu_custom_call" | custom-call | tf_op jit(solution)/shard_map/pallas_call | solution.py:781
  112.9 3.1 %shard_map.205 = (bf16[256,768]{1,0:T(8,128)(2,1)}, bf16[256,768]{1,0:T(8,128)(2,1)}, f32[24]{0:T(128)}, f32[24]{0:T(128)}, f32[24,2304]{1,0:T(8,128)}, /*index=...) custom-call(bf16[256,768]{1,0:T(8,128)(2,1)} %get-tuple-element.17.block_out, ...), custom_call_target="tpu_custom_call" | custom-call | tf_op jit(solution)/shard_map/pallas_call | solution.py:814
